TPU v7x, 32 devices: a whole 2x2x4 slice. The times are simulated.
32 devices in a mesh: fsdp: 16 (over z, y, core), ctx: 2 (over x).
Axes of the slice: x: 2, y: 2, z: 4, core: 2. Of those that a mesh axis runs over, the one named last changes fastest.
Arguments:
- hidden: bfloat16 [16, 512, 5120], P('fsdp', 'ctx'), may hold values from -6 to 6
- queries: bfloat16 [16, 512, 4096], P('fsdp', 'ctx'), may hold values from -300 to 300, as said below
- norm_gain: float32 [5120], replicated, may hold values from 0.1 to 1.9
- key_gain: float32 [128], replicated, may hold values from 0.1 to 1.9
- k_weight: bfloat16 [5120, 512], P('fsdp'), may hold values from -0.078125 to 0.078125
- v_weight: bfloat16 [5120, 512], P('fsdp'), may hold values from -0.078125 to 0.078125
- segment: int32 [16, 512], P('fsdp', 'ctx'), may hold values from 0 to 3, as said below
- position: int32 [16, 512], P('fsdp', 'ctx'), may hold values from 0 to 8191, as said below
Outputs:
- attended: bfloat16 [16, 512, 4096], P('fsdp', 'ctx')
Inputs may be any that keep to these rules, and one draw needn't show every extreme that they name: queries keep to the stated range. `segment`: in each stretch, read in the tokens' order, rollout numbers never fall; the tokens of a stretch lie in its slots in an order that keeps 256 slots on each index of ctx, one token of every 2 consecutive ones on each. `position`: within one rollout of a stretch positions rise by one from token to token.
All inputs are finite; a program needn't handle non-finite values.
Results may differ from a plain program's by a relative error of at most 0.0075.
The roundings to bfloat16 on the way count: a program that leaves them out, or rounds other values in their place, can miss the bound.
Values may be sent and summed in bfloat16 or wider, within the bound.
No kernel may reach another device: no remote copies, remote signals or barrier semaphores. Data moves between devices by JAX's collectives and lax.ppermute only.
A program may use at most 192 MiB of HBM per device.

v0:
```python
import functools
import math

import jax
import jax.numpy as jnp
import numpy as np
from jax import lax
from jax.experimental import pallas as pl
from jax.experimental.pallas import tpu as pltpu
from jax.sharding import Mesh
from jax.sharding import PartitionSpec as P

KVH = 4
HD = 128
G = 8
EPS = 1e-06
THETA = 1000000.0
MASKED = -1e30
VMEM_LIMIT = 24 * 2**20
NORM_ROWS = 64
WIDE = 4


def norm_kernel(chunks, hidden, gain, out, held, sems):
    steps = held.shape[0] // NORM_ROWS
    copies = []
    for i in range(steps):
        at = pl.ds(i * NORM_ROWS, NORM_ROWS)
        copies.append(pltpu.make_async_copy(hidden.at[at], held.at[at], sems.at[i]))
        copies[-1].start()
    for i, copy in enumerate(copies):
        copy.wait()
        at = pl.ds(i * NORM_ROWS, NORM_ROWS)
        inputs = held[at, :].astype(jnp.float32)
        scale = lax.rsqrt(jnp.mean(inputs * inputs, axis=-1, keepdims=True) + EPS)
        normed = (inputs * scale * gain[...]).astype(jnp.bfloat16)
        rows = normed.shape[1] // chunks
        for j in range(chunks):
            out[j, at, :] = normed[:, j * rows : (j + 1) * rows]


def project_kernel(groups, first, last, count, place, own, other, *rest):
    z, y, x = place[0], place[1], place[2]
    rest = list(rest)
    weight, lhs, sems = rest[-3:]
    waits = []
    for g, (k, near) in enumerate(groups):
        p = z ^ k
        chunk = p * 2 + (y if near else 1 - y)
        pairs = [
            (own.at[chunk], lhs.at[g, pl.ds(0, count)]),
            (other.at[chunk], lhs.at[g, pl.ds(count, count)]),
        ]
        if k == 0:
            pairs.append((rest.pop(0), weight.at[g]))
        else:
            pairs.append((rest.pop(0), weight.at[g, x]))
            pairs.append((rest.pop(0), weight.at[g, 1 - x]))
        copies = [
            pltpu.make_async_copy(source, target, sems.at[g, i])
            for i, (source, target) in enumerate(pairs)
        ]
        for copy in copies:
            copy.start()
        waits.append(copies)
    earlier = None if first else rest.pop(0)
    terms = [None, None]
    for g, copies in enumerate(waits):
        for copy in copies:
            copy.wait()
        for half in range(2):
            part = jnp.dot(lhs[g], weight[g, half], preferred_element_type=jnp.float32)
            terms[half] = part if terms[half] is None else terms[half] + part
    for half in range(2):
        if not first:
            terms[half] += earlier[half]
        if not last:
            rest[0][half] = terms[half]
    if not last:
        return
    cosine, sine, gain = rest[:3]
    outs = rest[3:5]
    for head in range(2):
        columns = slice(head * HD, (head + 1) * HD)
        for part, out in enumerate(outs):
            at = slice(part * count, (part + 1) * count)
            raw = terms[0][at, columns]
            normk = raw * lax.rsqrt(jnp.mean(raw * raw, axis=-1, keepdims=True) + EPS) * gain[...]
            turned = normk * cosine[at, :] + pltpu.roll(normk, HD // 2, 1) * sine[at, :]
            out[:, 2 * head * HD : (2 * head + 1) * HD] = turned.astype(jnp.bfloat16)
            out[:, (2 * head + 1) * HD : (2 * head + 2) * HD] = terms[1][at, columns].astype(
                jnp.bfloat16
            )


def mask_kernel(*refs):
    pieces, (bias, needs) = refs[:-2], refs[-2:]
    count = bias.shape[0]
    half_rows = count // 2
    seg_q, pos_q = (
        jnp.transpose(jnp.broadcast_to(pieces[0][i : i + 1, :], (half_rows, count)))
        for i in range(2)
    )
    half_width = len(pieces) * half_rows
    for half in range(2):
        for i, piece in enumerate(pieces):
            at = slice(half * half_rows, (half + 1) * half_rows)
            allowed = (piece[:1, at] == seg_q) & (piece[1:, at] <= pos_q)
            there = half * half_width + i * half_rows
            bias[:, there : there + half_rows] = jnp.where(allowed, 0.0, MASKED)
    for tile in range(2):
        rows = slice(tile * half_rows, (tile + 1) * half_rows)
        found = [
            jnp.max(bias[rows, half * half_width : (half + 1) * half_width]) == 0.0
            for half in range(2)
        ]
        needs[tile] = found[0].astype(jnp.int32) + 2 * found[1].astype(jnp.int32)


def attend_kernel(pieces, count, place, needs, queries, bias, *rest):
    sources, (out, keys, values) = rest[:pieces], rest[-3:]
    step = pl.program_id(0)
    tile_rows = count // 2
    length = pieces * tile_rows

    for head in range(2):

        @pl.when(step == head)
        def _():
            left = 2 * head * HD
            for i, source in enumerate(sources):
                for half in range(2):
                    here = slice(half * tile_rows, (half + 1) * tile_rows)
                    there = half * length + i * tile_rows
                    keys[there : there + tile_rows, :] = source[here, left : left + HD]
                    values[there : there + tile_rows, :] = source[here, left + HD : left + 2 * HD]

    factor = math.log2(math.e) / math.sqrt(HD)

    def tile_body(tile, low, high):
        rows = slice(tile * tile_rows, (tile + 1) * tile_rows)
        k, v, b = keys[low:high, :], values[low:high, :], bias[rows, low:high]

        def score(step):
            heads = range(step * WIDE, (step + 1) * WIDE)
            q = jnp.concatenate([queries[rows, g * HD : (g + 1) * HD] for g in heads], axis=0)
            return lax.dot_general(
                q, k, (((1,), (1,)), ((), ())), preferred_element_type=jnp.float32
            )

        ahead = score(0)
        for step in range(G // WIDE):
            scores = ahead.reshape(WIDE, tile_rows, high - low) + b[None]
            if step + 1 < G // WIDE:
                ahead = score(step + 1)
            top = jnp.max(scores, axis=-1, keepdims=True)
            weights = jnp.exp2((scores - top) * factor)
            total = jnp.sum(weights, axis=-1, keepdims=True)
            summed = jnp.dot(
                weights.astype(jnp.bfloat16).reshape(WIDE * tile_rows, high - low),
                v,
                preferred_element_type=jnp.float32,
            ).reshape(WIDE, tile_rows, HD)
            result = (summed * (1.0 / total)).astype(jnp.bfloat16)
            for i in range(WIDE):
                g = step * WIDE + i
                out[rows, g * HD : (g + 1) * HD] = result[i]

    for tile in range(2):
        for need, low, high in ((1, 0, length), (2, length, 2 * length), (3, 0, 2 * length)):

            @pl.when(needs[tile] == need)
            def _():
                tile_body(tile, low, high)


def swap(array, axis):
    return lax.ppermute(array, axis, [(0, 1), (1, 0)])


def on_device(
    sizes, hidden, queries, norm_gain, key_gain, k_weight, v_weight, segment, position
):
    chips_z, groups = sizes[0], sizes[3]
    count, width = hidden.shape[1:]
    own_rows = k_weight.shape[0]
    rows = 2 * own_rows
    chunks = 2 * chips_z
    m = 2 * groups
    z, y = lax.axis_index("z"), lax.axis_index("y")
    core, x = lax.axis_index("core"), lax.axis_index("x")
    bf16 = jnp.bfloat16
    whole = pl.BlockSpec(memory_space=pltpu.VMEM)
    params = pltpu.CompilerParams(vmem_limit_bytes=VMEM_LIMIT)

    def along_ctx(array, d, cross=False):
        pairs = []
        for c in range(2):
            for i in range(m):
                pairs.append((c * m + i, (c ^ int(cross)) * m + (i + d) % m))
        return lax.ppermute(array, ("core", "ctx", "x"), pairs)

    def columns(which):
        at = which * 2 * HD
        return jnp.stack(
            [lax.dynamic_slice_in_dim(w, at, 2 * HD, 1) for w in (k_weight, v_weight)]
        )

    taken = swap(columns(1 - core), "core")
    kept = columns(core)
    chip = lax.dynamic_update_slice(
        jnp.zeros((2, rows, 2 * HD), bf16), kept, (0, core * own_rows, 0)
    )
    chip = lax.dynamic_update_slice(chip, taken, (0, (1 - core) * own_rows, 0))
    hidden, segment, position, chip = lax.optimization_barrier((hidden, segment, position, chip))
    normed = pl.pallas_call(
        functools.partial(norm_kernel, chunks),
        out_shape=jax.ShapeDtypeStruct((chunks, count, rows), bf16),
        in_specs=[pl.BlockSpec(memory_space=pltpu.HBM), whole],
        out_specs=whole,
        scratch_shapes=[
            pltpu.VMEM((count, width), bf16),
            pltpu.SemaphoreType.DMA((count // NORM_ROWS,)),
        ],
        compiler_params=params,
        cost_estimate=pl.CostEstimate(
            flops=4 * count * width, bytes_accessed=4 * count * width, transcendentals=0
        ),
        name="norm",
    )(hidden[0], norm_gain[None])
    ints = jnp.concatenate([segment, position])
    ints_all = [ints] + [along_ctx(ints, d) for d in range(1, m)]
    ints_other = swap(ints, "core")

    def along_z(array, k):
        return lax.ppermute(array, "z", [(i, i ^ k) for i in range(chips_z)])

    tie = lax.optimization_barrier
    mine = {0: lax.dynamic_index_in_dim(chip, x, 0, keepdims=False)}
    across, beside, corner = {}, {}, {}
    chip_beside = swap(chip, "y")
    for k in range(1, chips_z):
        low = k & -k
        if k == 2:
            mine[0], normed = tie((mine[0], normed))
        mine[k] = along_z(mine[k - low], low)
        if k == 2:
            tied = (mine[k], across[1], beside[1], chip_beside, normed, ints_all, ints_other)
            tied = tie(tied)
            mine[k], across[1], beside[1], chip_beside, normed, ints_all, ints_other = tied
            normed_other = swap(normed, "core")
        elif k == 3:
            mine[k], beside[2], normed_other = tie((mine[k], beside[2], normed_other))
        elif k > 3:
            mine[k], beside[k - 1] = tie((mine[k], beside[k - 1]))
        across[k], beside[k] = swap(mine[k], "x"), swap(mine[k], "y")
    end = chips_z - 1
    for k in range(1, chips_z):
        corner[k] = swap(across[k], "y") if k == end else swap(beside[k], "x")

    where = jnp.concatenate([position[0], ints_other[1]]).astype(jnp.float32)
    half = HD // 2
    freq = np.exp(np.arange(half, dtype=np.float32) * np.float32(-2.0 * math.log(THETA) / HD))
    angle = where[:, None] * freq[None, :]
    cosine, sine = jnp.cos(angle), jnp.sin(angle)
    cosine = jnp.concatenate([cosine, cosine], axis=1)
    sine = jnp.concatenate([-sine, sine], axis=1)
    bias, needs = pl.pallas_call(
        mask_kernel,
        out_shape=[
            jax.ShapeDtypeStruct((count, m * count), jnp.float32),
            jax.ShapeDtypeStruct((2,), jnp.int32),
        ],
        in_specs=[whole] * m,
        out_specs=[whole, pl.BlockSpec(memory_space=pltpu.SMEM)],
        compiler_params=params,
        name="mask",
    )(*ints_all)

    place = jnp.stack([z, y, x]).astype(jnp.int32)
    acc_shape = jax.ShapeDtypeStruct((2, 2 * count, 2 * HD), jnp.float32)
    kv_shape = jax.ShapeDtypeStruct((count, 4 * HD), bf16)
    final = [(end - 1, False)]
    late = [(end, True)] + [(k, False) for k in range(1, chips_z) if k != end - 1]
    early = [(0, True), (0, False)] + [(k, True) for k in range(1, end)]
    acc = []
    for groups in (early, late, final):
        first, last = groups is early, groups is final
        arrays = []
        for k, near in groups:
            if k == 0:
                arrays.append(chip if near else chip_beside)
            else:
                arrays += [mine[k], across[k]] if near else [beside[k], corner[k]]
        anywhere = pl.BlockSpec(memory_space=pl.ANY)
        outs = pl.pallas_call(
            functools.partial(project_kernel, groups, first, last, count),
            out_shape=[kv_shape] * 2 if last else [acc_shape],
            in_specs=[pl.BlockSpec(memory_space=pltpu.SMEM)]
            + [anywhere] * (2 + len(arrays))
            + [whole] * (len(acc) + (3 if last else 0)),
            out_specs=[whole] * (2 if last else 1),
            scratch_shapes=[
                pltpu.VMEM((len(groups), 2, rows, 2 * HD), bf16),
                pltpu.VMEM((len(groups), 2 * count, rows), bf16),
                pltpu.SemaphoreType.DMA((len(groups), 4)),
            ],
            compiler_params=params,
            cost_estimate=pl.CostEstimate(
                flops=2 * 2 * count * rows * 4 * HD * len(groups),
                bytes_accessed=2 * rows * (4 * HD + 2 * count) * len(groups),
                transcendentals=0,
            ),
            name="project",
        )(
            place, normed, normed_other, *arrays, *acc,
            *((cosine, sine, key_gain[None]) if last else ()),
        )
        acc = [outs[-1]]

    kv_own, kv_other = outs
    result = None
    for cross, kv in enumerate((kv_own, kv_other)):
        sources = [kv if d == 0 and not cross else along_ctx(kv, d, cross) for d in range(m)]

        def block(step, place, needs, cross=cross):
            return (0, lax.rem(place[0] + cross, 2) * 2 + step)

        earlier = [] if result is None else [result]
        result = pl.pallas_call(
            functools.partial(attend_kernel, m, count),
            out_shape=jax.ShapeDtypeStruct((count, KVH * G * HD), bf16),
            grid_spec=pltpu.PrefetchScalarGridSpec(
                num_scalar_prefetch=2,
                grid=(2,),
                in_specs=[pl.BlockSpec((count, G * HD), block)]
                + [whole] * (1 + m)
                + [pl.BlockSpec(memory_space=pl.ANY)] * len(earlier),
                out_specs=pl.BlockSpec((count, G * HD), block),
                scratch_shapes=[
                    pltpu.VMEM((m * count, HD), bf16),
                    pltpu.VMEM((m * count, HD), bf16),
                ],
            ),
            input_output_aliases={4 + m: 0} if earlier else {},
            compiler_params=params,
            cost_estimate=pl.CostEstimate(
                flops=2 * count * m * count * KVH * G * HD,
                bytes_accessed=2 * count * KVH * G * HD,
                transcendentals=count * m * count * KVH * G // 2,
            ),
            name="attend",
        )(core.astype(jnp.int32)[None], needs, queries[0], bias, *sources, *earlier)
    return result[None]


def solution(mesh):
    n, m = mesh.shape["fsdp"], mesh.shape["ctx"]
    sizes = (n // 4, 2, 2, m // 2, 2)
    fine = Mesh(mesh.devices.reshape(sizes), ("z", "y", "core", "ctx", "x"))
    fsdp, ctx = ("z", "y", "core"), ("ctx", "x")
    placed = (
        P(fsdp, ctx, None),
        P(fsdp, ctx, None),
        P(),
        P(),
        P(fsdp, None),
        P(fsdp, None),
        P(fsdp, ctx),
        P(fsdp, ctx),
    )
    return jax.shard_map(
        functools.partial(on_device, sizes),
        mesh=fine,
        in_specs=placed,
        out_specs=P(fsdp, ctx, None),
        check_vma=False,
    )
```

profile of v0, /device:TPU:0, one launch (start us, length us, event | category | flops | bytes accessed | tf_op | source)
XLA Modules:
  0.0 91.7 jit_solution(8306503879579454480)
XLA Ops:
  0.0 1.2 %dynamic-slice_bitcast_fusion.1 = (bf16[1,320,256]{2,1,0:T(8,128)(2,1)S(1)}, bf16[1,320,256]{2,1,0:T(8,128)(2,1)S(1)}, bf16[1,320,256]{2,1,0:T(8,128)(2,1)S(1)}, bf16[1,320,256]{2,1,0:T(8,128)(2,1)S(1)}) fusion(bf16[320,512]{1,0:T(8,128)(2,1)} %param.14, s32[]{:T(128)S(6)} %select_n.20, s32[]{:T(128)S(6)} %select_n.18, bf16[320,512]{1,0:T(8,128)(2,1)} %param.13), kind=kLoop, calls=%fused_computation.7 | loop fusion | bytes 1310728 | tf_op jit(solution)/shard_map/stack | solution.py:205
  1.3 0.5 collective-permute-start
  1.9 1.2 %collective-permute-done = bf16[2,320,256]{2,1,0:T(8,128)(2,1)S(1)} collective-permute-done((bf16[2,320,256]{2,1,0:T(8,128)(2,1)S(1)}, bf16[2,320,256]{2,1,0:T(8,128)(2,1)S(1)}, u32[]{:S(2)}, u32[]{:S(2)}) %collective-permute-start) | collective-permute-done | bytes 327712 | tf_op jit(solution)/shard_map/ppermute | solution.py:178
  3.1 3.0 %collective-permute-start.2 = (bf16[640,256]{1,0:T(8,128)(2,1)S(1)}, bf16[640,256]{1,0:T(8,128)(2,1)S(1)}, u32[]{:S(2)}, u32[]{:S(2)}) collective-permute-start(bf16[640,256]{1,0:T(8,128)(2,1)S(1)} %dynamic-slice_bitcast_fusion), channel_id=1, source_target_pairs={{0,8},{8,0},{16,24},{24,16},{1,9},{9,1},{17,25},{25,17},{2,10},{10... | collective-permute-start | bytes 983048 | tf_op jit(solution)/shard_map/ppermute | solution.py:236
  6.1 1.5 %collective-permute-start.5 = (bf16[2,640,256]{2,1,0:T(8,128)(2,1)S(1)}, bf16[2,640,256]{2,1,0:T(8,128)(2,1)S(1)}, u32[]{:S(2)}, u32[]{:S(2)}) collective-permute-start(bf16[2,640,256]{2,1,0:T(8,128)(2,1)S(1)} %constant_dynamic-update-slice_fusion.rest_0_), channel_id=1, source_target_pairs={{0,4},{4,0},{1,5},{5,1},{2,6},{6,2},{3,7},{7,3},{8,12},{12,8},{9,1... | collective-permute-start | bytes 1966088 | tf_op jit(solution)/shard_map/ppermute | solution.py:178
  7.6 0.0 copy-start.14
  7.7 2.4 %norm.1.own = bf16[8,256,640]{2,1,0:T(8,128)(2,1)S(1)} custom-call(bf16[256,5120]{1,0:T(8,128)(2,1)S(1)} %bitcast.23, f32[1,5120]{1,0:T(1,128)S(1)} %bitcast.24), custom_call_target="tpu_custom_call" | custom-call | flops 5242880 | bytes 5242880 | tf_op jit(solution)/shard_map/norm/pallas_call | solution.py:216
  10.0 2.7 %collective-permute-start.1 = (bf16[640,256]{1,0:T(8,128)(2,1)S(1)}, bf16[640,256]{1,0:T(8,128)(2,1)}, u32[]{:S(2)}, u32[]{:S(2)}) collective-permute-start(bf16[640,256]{1,0:T(8,128)(2,1)S(1)} %dynamic-slice_bitcast_fusion), channel_id=1, source_target_pairs={{0,16},{8,24},{16,0},{24,8},{1,17},{9,25},{17,1},{25,9},{2,18},{10... | collective-permute-start | bytes 983048 | tf_op jit(solution)/shard_map/ppermute | solution.py:236
  12.7 4.6 %collective-permute-done.2.rest_2_ = bf16[640,256]{1,0:T(8,128)(2,1)S(1)} collective-permute-done((bf16[640,256]{1,0:T(8,128)(2,1)S(1)}, bf16[640,256]{1,0:T(8,128)(2,1)S(1)}, u32[]{:S(2)}, u32[]{:S(2)}) %collective-permute-start.2) | collective-permute-done | bytes 327712 | tf_op jit(solution)/shard_map/ppermute | solution.py:236
  17.3 1.7 %collective-permute-start.3 = (bf16[640,256]{1,0:T(8,128)(2,1)S(1)}, bf16[640,256]{1,0:T(8,128)(2,1)S(1)}, u32[]{:S(2)}, u32[]{:S(2)}) collective-permute-start(bf16[640,256]{1,0:T(8,128)(2,1)S(1)} %collective-permute-done.2.rest_2_), channel_id=1, source_target_pairs={{0,1},{1,0},{2,3},{3,2},{4,5},{5,4},{6,7},{7,6},{8,9},{9,8},{10,11... | collective-permute-start | bytes 983048 | tf_op jit(solution)/shard_map/ppermute | solution.py:178
  19.0 2.5 %collective-permute-start.4 = (bf16[640,256]{1,0:T(8,128)(2,1)S(1)}, bf16[640,256]{1,0:T(8,128)(2,1)S(1)}, u32[]{:S(2)}, u32[]{:S(2)}) collective-permute-start(bf16[640,256]{1,0:T(8,128)(2,1)S(1)} %collective-permute-done.2.rest_2_), channel_id=1, source_target_pairs={{0,4},{4,0},{1,5},{5,1},{2,6},{6,2},{3,7},{7,3},{8,12},{12,8},{9,1... | collective-permute-start | bytes 983048 | tf_op jit(solution)/shard_map/ppermute | solution.py:178
  21.5 0.7 copy-done.4
  22.3 0.6 collective-permute-start.6
  22.9 3.4 %collective-permute-done.6.refs_1_ = s32[2,256]{1,0:T(2,128)S(1)} collective-permute-done((s32[2,256]{1,0:T(2,128)S(1)}, s32[2,256]{1,0:T(2,128)S(1)}, u32[]{:S(2)}, u32[]{:S(2)}) %collective-permute-start.6) | collective-permute-done | bytes 2080 | tf_op jit(solution)/shard_map/ppermute | solution.py:201
  26.2 1.2 %collective-permute-done.7 = s32[2,256]{1,0:T(2,128)S(1)} collective-permute-done((s32[2,256]{1,0:T(2,128)S(1)}, s32[2,256]{1,0:T(2,128)S(1)}, u32[]{:S(2)}, u32[]{:S(2)}) %collective-permute-start.7) | collective-permute-done | bytes 2080 | tf_op jit(solution)/shard_map/ppermute | solution.py:178
  27.4 0.8 copy-done.8
  28.1 1.5 %collective-permute-done.4.rest_2_ = bf16[640,256]{1,0:T(8,128)(2,1)S(1)} collective-permute-done((bf16[640,256]{1,0:T(8,128)(2,1)S(1)}, bf16[640,256]{1,0:T(8,128)(2,1)S(1)}, u32[]{:S(2)}, u32[]{:S(2)}) %collective-permute-start.4) | collective-permute-done | bytes 327712 | tf_op jit(solution)/shard_map/ppermute | solution.py:178
  29.6 0.7 copy-done.6
  30.4 0.8 copy-done.2
  31.2 0.4 collective-permute-start.8
  31.6 1.6 %collective-permute-start.9 = (bf16[640,256]{1,0:T(8,128)(2,1)}, bf16[640,256]{1,0:T(8,128)(2,1)}, u32[]{:S(2)}, u32[]{:S(2)}) collective-permute-start(bf16[640,256]{1,0:T(8,128)(2,1)} %collective-permute-done.1.rest_4_), channel_id=1, source_target_pairs={{0,4},{4,0},{1,5},{5,1},{2,6},{6,2},{3,7},{7,3},{8,12},{12,8},{9,1... | collective-permute-start | bytes 983048 | tf_op jit(solution)/shard_map/ppermute | solution.py:178
  33.2 0.1 pad_add_fusion.1.place
  33.2 1.5 %collective-permute-start.16 = (bf16[640,256]{1,0:T(8,128)(2,1)}, bf16[640,256]{1,0:T(8,128)(2,1)S(1)}, u32[]{:S(2)}, u32[]{:S(2)}) collective-permute-start(bf16[640,256]{1,0:T(8,128)(2,1)} %collective-permute-done.1.rest_4_), channel_id=1, source_target_pairs={{0,1},{1,0},{2,3},{3,2},{4,5},{5,4},{6,7},{7,6},{8,9},{9,8},{10,11... | collective-permute-start | bytes 983048 | tf_op jit(solution)/shard_map/ppermute | solution.py:178
  34.7 0.5 collective-permute-start.13
  35.3 6.4 %collective-permute-done.8.rest_0_ = bf16[640,256]{1,0:T(8,128)(2,1)} collective-permute-done((bf16[640,256]{1,0:T(8,128)(2,1)}, bf16[640,256]{1,0:T(8,128)(2,1)}, u32[]{:S(2)}, u32[]{:S(2)}) %collective-permute-start.8) | collective-permute-done | bytes 327712 | tf_op jit(solution)/shard_map/ppermute | solution.py:236
  41.6 0.1 collective-permute-done.9.rest_0_
  41.7 1.6 %collective-permute-start.12 = (bf16[640,256]{1,0:T(8,128)(2,1)}, bf16[640,256]{1,0:T(8,128)(2,1)S(1)}, u32[]{:S(2)}, u32[]{:S(2)}) collective-permute-start(bf16[640,256]{1,0:T(8,128)(2,1)} %collective-permute-done.8.rest_0_), channel_id=1, source_target_pairs={{0,1},{1,0},{2,3},{3,2},{4,5},{5,4},{6,7},{7,6},{8,9},{9,8},{10,11... | collective-permute-start | bytes 983048 | tf_op jit(solution)/shard_map/ppermute | solution.py:178
  43.3 1.0 %fusion = (f32[512,64]{1,0:T(8,128)S(1)}, f32[512,64]{1,0:T(8,128)S(1)}, f32[512,64]{1,0:T(8,128)S(1)}) fusion(f32[64]{0:T(128)S(1)} %copy-done.14, f32[512]{0:T(512)S(1)} %add_convert_fusion), kind=kLoop, calls=%fused_computation.11 | loop fusion | flops 65536 | bytes 395520 | tf_op jit(solution)/shard_map/neg | solution.py:267
  44.3 1.6 %collective-permute-start.14 = (bf16[640,256]{1,0:T(8,128)(2,1)}, bf16[640,256]{1,0:T(8,128)(2,1)S(1)}, u32[]{:S(2)}, u32[]{:S(2)}) collective-permute-start(bf16[640,256]{1,0:T(8,128)(2,1)} %collective-permute-done.8.rest_0_), channel_id=1, source_target_pairs={{0,4},{4,0},{1,5},{5,1},{2,6},{6,2},{3,7},{7,3},{8,12},{12,8},{9,1... | collective-permute-start | bytes 983048 | tf_op jit(solution)/shard_map/ppermute | solution.py:178
  45.9 11.2 %collective-permute-done.12.rest_1_ = bf16[640,256]{1,0:T(8,128)(2,1)S(1)} collective-permute-done((bf16[640,256]{1,0:T(8,128)(2,1)}, bf16[640,256]{1,0:T(8,128)(2,1)S(1)}, u32[]{:S(2)}, u32[]{:S(2)}) %collective-permute-start.12) | collective-permute-done | bytes 327712 | tf_op jit(solution)/shard_map/ppermute | solution.py:178
  57.1 0.4 collective-permute-start.15
  57.5 0.1 pad_maximum_fusion.1.rest_3_
  57.6 1.6 %collective-permute-start.11 = (bf16[640,256]{1,0:T(8,128)(2,1)}, bf16[640,256]{1,0:T(8,128)(2,1)S(1)}, u32[]{:S(2)}, u32[]{:S(2)}) collective-permute-start(bf16[640,256]{1,0:T(8,128)(2,1)} %collective-permute-done.9.rest_0_), channel_id=1, source_target_pairs={{0,1},{1,0},{2,3},{3,2},{4,5},{5,4},{6,7},{7,6},{8,9},{9,8},{10,11... | collective-permute-start | bytes 983048 | tf_op jit(solution)/shard_map/ppermute | solution.py:178
  59.3 0.1 pad_maximum_fusion.2.rest_4_
  59.4 1.1 %copy-done.3 = bf16[2,640,256]{2,1,0:T(8,128)(2,1)S(1)} copy-done((bf16[2,640,256]{2,1,0:T(8,128)(2,1)S(1)}, bf16[2,640,256]{2,1,0:T(8,128)(2,1)}, u32[]{:S(2)}) %copy-start.3) | copy-done | bytes 655384
  60.5 1.0 %copy-done.5 = bf16[640,256]{1,0:T(8,128)(2,1)S(1)} copy-done((bf16[640,256]{1,0:T(8,128)(2,1)S(1)}, bf16[640,256]{1,0:T(8,128)(2,1)}, u32[]{:S(2)}) %copy-start.5) | copy-done | bytes 327704
  61.5 1.0 %copy-done.9 = bf16[640,256]{1,0:T(8,128)(2,1)S(1)} copy-done((bf16[640,256]{1,0:T(8,128)(2,1)S(1)}, bf16[640,256]{1,0:T(8,128)(2,1)}, u32[]{:S(2)}) %copy-start.9) | copy-done | bytes 327704
  62.5 4.0 %project.3.rest_6_ = f32[2,512,256]{2,1,0:T(8,128)S(1)} custom-call(s32[3]{0:T(128)S(1)} %pad_add_fusion.1.place, bf16[8,256,640]{2,1,0:T(8,128)(2,1)S(1)} %norm.1.own, bf16[8,256,640]{2,1,0:T(8,128)(2,1)} %collective-permute-done.10.other, bf16[2,640,256]{2,1,0:T(8,128)(2,1)S(1)} %constant_dynamic-update-slice_fusion.rest_0_, ...), custom_call_target="tpu_custom_call" | custom-call | flops 1342177280 | bytes 5242880 | tf_op jit(solution)/shard_map/project/pallas_call | solution.py:296
  66.5 0.0 copy-start.11
  66.5 3.4 %project.4.rest_2_ = f32[2,512,256]{2,1,0:T(8,128)S(1)} custom-call(s32[3]{0:T(128)S(1)} %pad_add_fusion.1.place, bf16[8,256,640]{2,1,0:T(8,128)(2,1)S(1)} %norm.1.own, bf16[8,256,640]{2,1,0:T(8,128)(2,1)} %collective-permute-done.10.other, bf16[640,256]{1,0:T(8,128)(2,1)} %collective-permute-done.8.rest_0_, ...), custom_call_target="tpu_custom_call" | custom-call | flops 1006632960 | bytes 3932160 | tf_op jit(solution)/shard_map/project/pallas_call | solution.py:296
  70.0 0.0 copy-start
  70.0 2.8 %project.5 = (bf16[256,512]{1,0:T(8,128)(2,1)S(1)}, bf16[256,512]{1,0:T(8,128)(2,1)S(1)}) custom-call(s32[3]{0:T(128)S(1)} %pad_add_fusion.1.place, bf16[8,256,640]{2,1,0:T(8,128)(2,1)S(1)} %norm.1.own, bf16[8,256,640]{2,1,0:T(8,128)(2,1)} %collective-permute-done.10.other, bf16[640,256]{1,0:T(8,128)(2,1)} %collective-permute-done.9.rest_0_, ...), custom_call_target="tpu_custom_call" | custom-call | flops 335544320 | bytes 1310720 | tf_op jit(solution)/shard_map/project/pallas_call | solution.py:296
  72.8 0.8 collective-permute-start.19
  73.6 1.4 %collective-permute-start.18 = (bf16[256,512]{1,0:T(8,128)(2,1)S(1)}, bf16[256,512]{1,0:T(8,128)(2,1)S(1)}, u32[]{:S(2)}, u32[]{:S(2)}) collective-permute-start(bf16[256,512]{1,0:T(8,128)(2,1)S(1)} %get-tuple-element.45), channel_id=1, source_target_pairs={{0,3},{1,2},{2,1},{3,0},{4,7},{5,6},{6,5},{7,4},{8,11},{9,10},{10,... | collective-permute-start | bytes 786440 | tf_op jit(solution)/shard_map/ppermute | solution.py:201
  75.0 0.9 mask.1
  75.9 6.2 %collective-permute-done.19.rest_1_ = bf16[256,512]{1,0:T(8,128)(2,1)S(1)} collective-permute-done((bf16[256,512]{1,0:T(8,128)(2,1)S(1)}, bf16[256,512]{1,0:T(8,128)(2,1)S(1)}, u32[]{:S(2)}, u32[]{:S(2)}) %collective-permute-start.19) | collective-permute-done | bytes 262176 | tf_op jit(solution)/shard_map/ppermute | solution.py:201
  82.1 4.7 %attend.2.rest_2_ = bf16[256,4096]{1,0:T(8,128)(2,1)} custom-call(s32[1]{0:T(128)} %bitcast.place, s32[2]{0:T(128)S(1)} %get-tuple-element.34.needs, bf16[256,4096]{1,0:T(8,128)(2,1)S(1)} %bitcast.21, f32[256,512]{1,0:T(8,128)S(1)} %get-tuple-element.35.bias, bf16[256,512]{1,0:T(8,128)(2,1)S(1)} %get-tuple-element.46.rest_0_, ...), custom_call_target="tpu_custom_call" | custom-call | flops 1073741824 | bytes 2097152 | tf_op jit(solution)/shard_map/attend/pallas_call | solution.py:330
  86.8 4.9 %attend.3 = bf16[256,4096]{1,0:T(8,128)(2,1)} custom-call(s32[1]{0:T(128)} %bitcast.place, s32[2]{0:T(128)S(1)} %get-tuple-element.34.needs, bf16[256,4096]{1,0:T(8,128)(2,1)S(1)} %bitcast.22, f32[256,512]{1,0:T(8,128)S(1)} %get-tuple-element.35.bias, bf16[256,512]{1,0:T(8,128)(2,1)S(1)} %collective-permute-done.17.rest_0_, ...), custom_call_target="tpu_custom_call", output_to_operand_aliasing={{}: (6, {})} | custom-call | flops 1073741824 | bytes 2097152 | tf_op jit(solution)/shard_map/attend/pallas_call | solution.py:330
  (42 shorter events, 0.3 us)
Async XLA Ops:
  0.0 7.6 %copy-start.10 = (f32[5120]{0:T(1024)S(1)}, f32[5120]{0:T(1024)}, u32[]{:S(2)}) copy-start(f32[5120]{0:T(1024)} %param.11) | copy-start | bytes 61444
  1.3 1.8 %collective-permute-start = (bf16[2,320,256]{2,1,0:T(8,128)(2,1)S(1)}, bf16[2,320,256]{2,1,0:T(8,128)(2,1)S(1)}, u32[]{:S(2)}, u32[]{:S(2)}) collective-permute-start(bf16[2,320,256]{2,1,0:T(8,128)(2,1)S(1)} %pad_maximum_fusion), channel_id=1, source_target_pairs={{0,2},{2,0},{1,3},{3,1},{4,6},{6,4},{5,7},{7,5},{8,10},{10,8},{9,1... | collective-permute-start | bytes 983048 | tf_op jit(solution)/shard_map/ppermute | solution.py:178
  1.8 5.9 %copy-start.1 = (bf16[1,256,5120]{2,1,0:T(8,128)(2,1)S(1)}, bf16[1,256,5120]{2,1,0:T(8,128)(2,1)}, u32[]{:S(2)}) copy-start(bf16[1,256,5120]{2,1,0:T(8,128)(2,1)} %param.9) | copy-start | bytes 7864324
  3.1 14.2 %collective-permute-start.2 = (bf16[640,256]{1,0:T(8,128)(2,1)S(1)}, bf16[640,256]{1,0:T(8,128)(2,1)S(1)}, u32[]{:S(2)}, u32[]{:S(2)}) collective-permute-start(bf16[640,256]{1,0:T(8,128)(2,1)S(1)} %dynamic-slice_bitcast_fusion), channel_id=1, source_target_pairs={{0,8},{8,0},{16,24},{24,16},{1,9},{9,1},{17,25},{25,17},{2,10},{10... | collective-permute-start | bytes 983048 | tf_op jit(solution)/shard_map/ppermute | solution.py:236
  6.1 23.5 %collective-permute-start.5 = (bf16[2,640,256]{2,1,0:T(8,128)(2,1)S(1)}, bf16[2,640,256]{2,1,0:T(8,128)(2,1)S(1)}, u32[]{:S(2)}, u32[]{:S(2)}) collective-permute-start(bf16[2,640,256]{2,1,0:T(8,128)(2,1)S(1)} %constant_dynamic-update-slice_fusion.rest_0_), channel_id=1, source_target_pairs={{0,4},{4,0},{1,5},{5,1},{2,6},{6,2},{3,7},{7,3},{8,12},{12,8},{9,1... | collective-permute-start | bytes 1966088 | tf_op jit(solution)/shard_map/ppermute | solution.py:178
  7.6 14.6 %copy-start.12 = (s32[1,256]{1,0:T(1,128)S(1)}, s32[1,256]{1,0:T(1,128)}, u32[]{:S(2)}) copy-start(s32[1,256]{1,0:T(1,128)} %param.16) | copy-start | bytes 3076
  7.6 14.6 %copy-start.13 = (s32[1,256]{1,0:T(1,128)S(1)}, s32[1,256]{1,0:T(1,128)}, u32[]{:S(2)}) copy-start(s32[1,256]{1,0:T(1,128)} %param.15) | copy-start | bytes 3076
  7.6 35.7 %copy-start.14 = (f32[64]{0:T(128)S(1)}, f32[64]{0:T(128)}, u32[]{:S(2)}) copy-start(f32[64]{0:T(128)} %constant.43) | copy-start | bytes 772
  10.0 17.4 %collective-permute-start.1 = (bf16[640,256]{1,0:T(8,128)(2,1)S(1)}, bf16[640,256]{1,0:T(8,128)(2,1)}, u32[]{:S(2)}, u32[]{:S(2)}) collective-permute-start(bf16[640,256]{1,0:T(8,128)(2,1)S(1)} %dynamic-slice_bitcast_fusion), channel_id=1, source_target_pairs={{0,16},{8,24},{16,0},{24,8},{1,17},{9,25},{17,1},{25,9},{2,18},{10... | collective-permute-start | bytes 983048 | tf_op jit(solution)/shard_map/ppermute | solution.py:236
  17.3 10.1 %collective-permute-start.3 = (bf16[640,256]{1,0:T(8,128)(2,1)S(1)}, bf16[640,256]{1,0:T(8,128)(2,1)S(1)}, u32[]{:S(2)}, u32[]{:S(2)}) collective-permute-start(bf16[640,256]{1,0:T(8,128)(2,1)S(1)} %collective-permute-done.2.rest_2_), channel_id=1, source_target_pairs={{0,1},{1,0},{2,3},{3,2},{4,5},{5,4},{6,7},{7,6},{8,9},{9,8},{10,11... | collective-permute-start | bytes 983048 | tf_op jit(solution)/shard_map/ppermute | solution.py:178
  19.0 10.7 %collective-permute-start.4 = (bf16[640,256]{1,0:T(8,128)(2,1)S(1)}, bf16[640,256]{1,0:T(8,128)(2,1)S(1)}, u32[]{:S(2)}, u32[]{:S(2)}) collective-permute-start(bf16[640,256]{1,0:T(8,128)(2,1)S(1)} %collective-permute-done.2.rest_2_), channel_id=1, source_target_pairs={{0,4},{4,0},{1,5},{5,1},{2,6},{6,2},{3,7},{7,3},{8,12},{12,8},{9,1... | collective-permute-start | bytes 983048 | tf_op jit(solution)/shard_map/ppermute | solution.py:178
  21.5 0.7 copy-start.4
  22.3 4.0 %collective-permute-start.6 = (s32[2,256]{1,0:T(2,128)S(1)}, s32[2,256]{1,0:T(2,128)S(1)}, u32[]{:S(2)}, u32[]{:S(2)}) collective-permute-start(s32[2,256]{1,0:T(2,128)S(1)} %pad_add_fusion.refs_0_), channel_id=1, source_target_pairs={{0,1},{1,0},{2,3},{3,2},{4,5},{5,4},{6,7},{7,6},{8,9},{9,8},{10,11... | collective-permute-start | bytes 6152 | tf_op jit(solution)/shard_map/ppermute | solution.py:201
  26.2 1.2 %collective-permute-start.7 = (s32[2,256]{1,0:T(2,128)S(1)}, s32[2,256]{1,0:T(2,128)S(1)}, u32[]{:S(2)}, u32[]{:S(2)}) collective-permute-start(s32[2,256]{1,0:T(2,128)S(1)} %pad_add_fusion.refs_0_), channel_id=1, source_target_pairs={{0,2},{2,0},{1,3},{3,1},{4,6},{6,4},{5,7},{7,5},{8,10},{10,8},{9,1... | collective-permute-start | bytes 6152 | tf_op jit(solution)/shard_map/ppermute | solution.py:178
  27.4 0.8 copy-start.8
  29.6 0.7 copy-start.6
  30.4 0.8 copy-start.2
  31.2 10.5 %collective-permute-start.10 = (bf16[8,256,640]{2,1,0:T(8,128)(2,1)S(1)}, bf16[8,256,640]{2,1,0:T(8,128)(2,1)}, u32[]{:S(2)}, u32[]{:S(2)}) collective-permute-start(bf16[8,256,640]{2,1,0:T(8,128)(2,1)S(1)} %norm.1.own), channel_id=1, source_target_pairs={{0,2},{2,0},{1,3},{3,1},{4,6},{6,4},{5,7},{7,5},{8,10},{10,8},{9,1... | collective-permute-start | bytes 7864328 | tf_op jit(solution)/shard_map/ppermute | solution.py:178
  31.2 10.4 %collective-permute-start.8 = (bf16[640,256]{1,0:T(8,128)(2,1)}, bf16[640,256]{1,0:T(8,128)(2,1)}, u32[]{:S(2)}, u32[]{:S(2)}) collective-permute-start(bf16[640,256]{1,0:T(8,128)(2,1)} %collective-permute-done.1.rest_4_), channel_id=1, source_target_pairs={{0,8},{8,0},{16,24},{24,16},{1,9},{9,1},{17,25},{25,17},{2,10},{10... | collective-permute-start | bytes 983048 | tf_op jit(solution)/shard_map/ppermute | solution.py:236
  31.6 10.2 %collective-permute-start.9 = (bf16[640,256]{1,0:T(8,128)(2,1)}, bf16[640,256]{1,0:T(8,128)(2,1)}, u32[]{:S(2)}, u32[]{:S(2)}) collective-permute-start(bf16[640,256]{1,0:T(8,128)(2,1)} %collective-permute-done.1.rest_4_), channel_id=1, source_target_pairs={{0,4},{4,0},{1,5},{5,1},{2,6},{6,2},{3,7},{7,3},{8,12},{12,8},{9,1... | collective-permute-start | bytes 983048 | tf_op jit(solution)/shard_map/ppermute | solution.py:178
  33.2 26.2 %collective-permute-start.16 = (bf16[640,256]{1,0:T(8,128)(2,1)}, bf16[640,256]{1,0:T(8,128)(2,1)S(1)}, u32[]{:S(2)}, u32[]{:S(2)}) collective-permute-start(bf16[640,256]{1,0:T(8,128)(2,1)} %collective-permute-done.1.rest_4_), channel_id=1, source_target_pairs={{0,1},{1,0},{2,3},{3,2},{4,5},{5,4},{6,7},{7,6},{8,9},{9,8},{10,11... | collective-permute-start | bytes 983048 | tf_op jit(solution)/shard_map/ppermute | solution.py:178
  34.7 31.7 %collective-permute-start.13 = (bf16[640,256]{1,0:T(8,128)(2,1)}, bf16[640,256]{1,0:T(8,128)(2,1)S(1)}, u32[]{:S(2)}, u32[]{:S(2)}) collective-permute-start(bf16[640,256]{1,0:T(8,128)(2,1)} %copy-done.6), channel_id=1, source_target_pairs={{0,1},{1,0},{2,3},{3,2},{4,5},{5,4},{6,7},{7,6},{8,9},{9,8},{10,11... | collective-permute-start | bytes 983048 | tf_op jit(solution)/shard_map/ppermute | solution.py:178
  41.7 15.3 %collective-permute-start.12 = (bf16[640,256]{1,0:T(8,128)(2,1)}, bf16[640,256]{1,0:T(8,128)(2,1)S(1)}, u32[]{:S(2)}, u32[]{:S(2)}) collective-permute-start(bf16[640,256]{1,0:T(8,128)(2,1)} %collective-permute-done.8.rest_0_), channel_id=1, source_target_pairs={{0,1},{1,0},{2,3},{3,2},{4,5},{5,4},{6,7},{7,6},{8,9},{9,8},{10,11... | collective-permute-start | bytes 983048 | tf_op jit(solution)/shard_map/ppermute | solution.py:178
  44.3 22.2 %collective-permute-start.14 = (bf16[640,256]{1,0:T(8,128)(2,1)}, bf16[640,256]{1,0:T(8,128)(2,1)S(1)}, u32[]{:S(2)}, u32[]{:S(2)}) collective-permute-start(bf16[640,256]{1,0:T(8,128)(2,1)} %collective-permute-done.8.rest_0_), channel_id=1, source_target_pairs={{0,4},{4,0},{1,5},{5,1},{2,6},{6,2},{3,7},{7,3},{8,12},{12,8},{9,1... | collective-permute-start | bytes 983048 | tf_op jit(solution)/shard_map/ppermute | solution.py:178
  57.1 9.4 %collective-permute-start.15 = (bf16[640,256]{1,0:T(8,128)(2,1)S(1)}, bf16[640,256]{1,0:T(8,128)(2,1)S(1)}, u32[]{:S(2)}, u32[]{:S(2)}) collective-permute-start(bf16[640,256]{1,0:T(8,128)(2,1)S(1)} %collective-permute-done.12.rest_1_), channel_id=1, source_target_pairs={{0,4},{4,0},{1,5},{5,1},{2,6},{6,2},{3,7},{7,3},{8,12},{12,8},{9,1... | collective-permute-start | bytes 983048 | tf_op jit(solution)/shard_map/ppermute | solution.py:178
  57.6 12.3 %collective-permute-start.11 = (bf16[640,256]{1,0:T(8,128)(2,1)}, bf16[640,256]{1,0:T(8,128)(2,1)S(1)}, u32[]{:S(2)}, u32[]{:S(2)}) collective-permute-start(bf16[640,256]{1,0:T(8,128)(2,1)} %collective-permute-done.9.rest_0_), channel_id=1, source_target_pairs={{0,1},{1,0},{2,3},{3,2},{4,5},{5,4},{6,7},{7,6},{8,9},{9,8},{10,11... | collective-permute-start | bytes 983048 | tf_op jit(solution)/shard_map/ppermute | solution.py:178
  59.4 1.1 %copy-start.3 = (bf16[2,640,256]{2,1,0:T(8,128)(2,1)S(1)}, bf16[2,640,256]{2,1,0:T(8,128)(2,1)}, u32[]{:S(2)}) copy-start(bf16[2,640,256]{2,1,0:T(8,128)(2,1)} %copy-done.2) | copy-start | bytes 1966084
  60.5 1.0 %copy-start.5 = (bf16[640,256]{1,0:T(8,128)(2,1)S(1)}, bf16[640,256]{1,0:T(8,128)(2,1)}, u32[]{:S(2)}) copy-start(bf16[640,256]{1,0:T(8,128)(2,1)} %copy-done.4) | copy-start | bytes 983044
  61.5 1.0 %copy-start.9 = (bf16[640,256]{1,0:T(8,128)(2,1)S(1)}, bf16[640,256]{1,0:T(8,128)(2,1)}, u32[]{:S(2)}) copy-start(bf16[640,256]{1,0:T(8,128)(2,1)} %copy-done.8) | copy-start | bytes 983044
  62.5 4.1 %copy-start.7 = (bf16[640,256]{1,0:T(8,128)(2,1)S(1)}, bf16[640,256]{1,0:T(8,128)(2,1)}, u32[]{:S(2)}) copy-start(bf16[640,256]{1,0:T(8,128)(2,1)} %copy-done.6) | copy-start | bytes 983044
  66.5 3.5 %copy-start.11 = (f32[128]{0:T(128)S(1)}, f32[128]{0:T(128)}, u32[]{:S(2)}) copy-start(f32[128]{0:T(128)} %param.12) | copy-start | bytes 1540
  70.0 12.1 %copy-start = (bf16[1,256,4096]{2,1,0:T(8,128)(2,1)S(1)}, bf16[1,256,4096]{2,1,0:T(8,128)(2,1)}, u32[]{:S(2)}) copy-start(bf16[1,256,4096]{2,1,0:T(8,128)(2,1)} %param.10) | copy-start | bytes 6291460
  72.8 9.3 %collective-permute-start.19 = (bf16[256,512]{1,0:T(8,128)(2,1)S(1)}, bf16[256,512]{1,0:T(8,128)(2,1)S(1)}, u32[]{:S(2)}, u32[]{:S(2)}) collective-permute-start(bf16[256,512]{1,0:T(8,128)(2,1)S(1)} %get-tuple-element.46.rest_0_), channel_id=1, source_target_pairs={{0,1},{1,0},{2,3},{3,2},{4,5},{5,4},{6,7},{7,6},{8,9},{9,8},{10,11... | collective-permute-start | bytes 786440 | tf_op jit(solution)/shard_map/ppermute | solution.py:201
  73.6 13.2 %collective-permute-start.17 = (bf16[256,512]{1,0:T(8,128)(2,1)S(1)}, bf16[256,512]{1,0:T(8,128)(2,1)S(1)}, u32[]{:S(2)}, u32[]{:S(2)}) collective-permute-start(bf16[256,512]{1,0:T(8,128)(2,1)S(1)} %get-tuple-element.45), channel_id=1, source_target_pairs={{0,2},{1,3},{2,0},{3,1},{4,6},{5,7},{6,4},{7,5},{8,10},{9,11},{10,... | collective-permute-start | bytes 786440 | tf_op jit(solution)/shard_map/ppermute | solution.py:201
  73.6 13.2 %collective-permute-start.18 = (bf16[256,512]{1,0:T(8,128)(2,1)S(1)}, bf16[256,512]{1,0:T(8,128)(2,1)S(1)}, u32[]{:S(2)}, u32[]{:S(2)}) collective-permute-start(bf16[256,512]{1,0:T(8,128)(2,1)S(1)} %get-tuple-element.45), channel_id=1, source_target_pairs={{0,3},{1,2},{2,1},{3,0},{4,7},{5,6},{6,5},{7,4},{8,11},{9,10},{10,... | collective-permute-start | bytes 786440 | tf_op jit(solution)/shard_map/ppermute | solution.py:201
where the time goes:
time: 92 us; the launch traced here: 91.7 us
  waiting for transfers between devices  35.6 us (39%)
  starting transfers between devices  23.9 us (26%)
  Pallas kernels  23.1 us (25%)
  local copies, waits for them, and re-layouts  7.44 us (8%)
  other arithmetic  1.41 us (2%)
    ppermute x13, starting transfers between devices, swap(): return lax.ppermute(array, axis, [(0, 1), (1, 0)])  15.1 us
    ppermute x13, waiting for transfers between devices, swap(): return lax.ppermute(array, axis, [(0, 1), (1, 0)])  15.1 us
    ppermute x3, waiting for transfers between devices, along_z(): return lax.ppermute(array, 'z', [(i, i ^ k) for i in range(chips_z)])  11 us
    pallas_call x3, Pallas kernels, on_device(): pl.pallas_call(functools.partial(project_kernel, groups, first, last, cou...  10.2 us
    ppermute x4, waiting for transfers between devices, along_ctx(): return lax.ppermute(array, ('core', 'ctx', 'x'), pairs)  9.59 us
    pallas_call x2, Pallas kernels, on_device(): pl.pallas_call(functools.partial(attend_kernel, m, count), out_shape=jax....  9.57 us
    unnamed x30, local copies, waits for them, and re-layouts  6.12 us
    ppermute x3, starting transfers between devices, along_z(): return lax.ppermute(array, 'z', [(i, i ^ k) for i in range(chips_z)])  6.02 us
  transfers between devices with their start and end apart: 20, of which 9 were waited for; matrix products, arithmetic and copies ran while one was open for 2% of the time, Pallas kernels for 17%

commit v1 on v0

--- a/solution.py
+++ b/solution.py
@@ -40,22 +40,25 @@
 
 
 def project_kernel(groups, first, last, count, place, own, other, *rest):
-    z, y, x = place[0], place[1], place[2]
+    chips_z = own.shape[0] // 2
+    y, x, spot = place[0], place[1], place[2]
     rest = list(rest)
     weight, lhs, sems = rest[-3:]
     waits = []
     for g, (k, near) in enumerate(groups):
-        p = z ^ k
-        chunk = p * 2 + (y if near else 1 - y)
+        i = lax.rem(spot - k + chips_z, chips_z)
+        chunk = (i ^ (i >> 1)) * 2 + (y if near else 1 - y)
         pairs = [
             (own.at[chunk], lhs.at[g, pl.ds(0, count)]),
             (other.at[chunk], lhs.at[g, pl.ds(count, count)]),
         ]
         if k == 0:
-            pairs.append((rest.pop(0), weight.at[g]))
+            both = rest.pop(0)
+            pairs += [(both.at[h], weight.at[g, :, pl.ds(h * HD, HD)]) for h in range(2)]
         else:
-            pairs.append((rest.pop(0), weight.at[g, x]))
-            pairs.append((rest.pop(0), weight.at[g, 1 - x]))
+            for h in (x, 1 - x):
+                at = pl.ds(pl.multiple_of(h * HD, HD), HD)
+                pairs.append((rest.pop(0), weight.at[g, :, at]))
         copies = [
             pltpu.make_async_copy(source, target, sems.at[g, i])
             for i, (source, target) in enumerate(pairs)
@@ -63,34 +66,23 @@
         for copy in copies:
             copy.start()
         waits.append(copies)
-    earlier = None if first else rest.pop(0)
-    terms = [None, None]
+    total = None if first else rest.pop(0)[...]
     for g, copies in enumerate(waits):
         for copy in copies:
             copy.wait()
-        for half in range(2):
-            part = jnp.dot(lhs[g], weight[g, half], preferred_element_type=jnp.float32)
-            terms[half] = part if terms[half] is None else terms[half] + part
-    for half in range(2):
-        if not first:
-            terms[half] += earlier[half]
-        if not last:
-            rest[0][half] = terms[half]
+        part = jnp.dot(lhs[g], weight[g], preferred_element_type=jnp.float32)
+        total = part if total is None else total + part
     if not last:
+        rest[0][...] = total
         return
     cosine, sine, gain = rest[:3]
-    outs = rest[3:5]
-    for head in range(2):
-        columns = slice(head * HD, (head + 1) * HD)
-        for part, out in enumerate(outs):
-            at = slice(part * count, (part + 1) * count)
-            raw = terms[0][at, columns]
-            normk = raw * lax.rsqrt(jnp.mean(raw * raw, axis=-1, keepdims=True) + EPS) * gain[...]
-            turned = normk * cosine[at, :] + pltpu.roll(normk, HD // 2, 1) * sine[at, :]
-            out[:, 2 * head * HD : (2 * head + 1) * HD] = turned.astype(jnp.bfloat16)
-            out[:, (2 * head + 1) * HD : (2 * head + 2) * HD] = terms[1][at, columns].astype(
-                jnp.bfloat16
-            )
+    for part, out in enumerate(rest[3:5]):
+        at = slice(part * count, (part + 1) * count)
+        raw = total[at, :HD]
+        normk = raw * lax.rsqrt(jnp.mean(raw * raw, axis=-1, keepdims=True) + EPS) * gain[...]
+        turned = normk * cosine[at, :] + pltpu.roll(normk, HD // 2, 1) * sine[at, :]
+        out[:, :HD] = turned.astype(jnp.bfloat16)
+        out[:, HD:] = total[at, HD:].astype(jnp.bfloat16)
 
 
 def mask_kernel(*refs):
@@ -118,7 +110,7 @@
 
 
 def attend_kernel(pieces, count, place, needs, queries, bias, *rest):
-    sources, (out, keys, values) = rest[:pieces], rest[-3:]
+    sources, (out, keys, values) = rest[: 2 * pieces], rest[-3:]
     step = pl.program_id(0)
     tile_rows = count // 2
     length = pieces * tile_rows
@@ -127,13 +119,13 @@
 
         @pl.when(step == head)
         def _():
-            left = 2 * head * HD
-            for i, source in enumerate(sources):
+            for i in range(pieces):
+                source = sources[head * pieces + i]
                 for half in range(2):
                     here = slice(half * tile_rows, (half + 1) * tile_rows)
                     there = half * length + i * tile_rows
-                    keys[there : there + tile_rows, :] = source[here, left : left + HD]
-                    values[there : there + tile_rows, :] = source[here, left + HD : left + 2 * HD]
+                    keys[there : there + tile_rows, :] = source[here, :HD]
+                    values[there : there + tile_rows, :] = source[here, HD:]
 
     factor = math.log2(math.e) / math.sqrt(HD)
 
@@ -232,31 +224,42 @@
     ints_all = [ints] + [along_ctx(ints, d) for d in range(1, m)]
     ints_other = swap(ints, "core")
 
-    def along_z(array, k):
-        return lax.ppermute(array, "z", [(i, i ^ k) for i in range(chips_z)])
-
+    order = [i ^ (i >> 1) for i in range(chips_z)]
+    ring = [(order[i], order[(i + 1) % chips_z]) for i in range(chips_z)]
     tie = lax.optimization_barrier
-    mine = {0: lax.dynamic_index_in_dim(chip, x, 0, keepdims=False)}
-    across, beside, corner = {}, {}, {}
-    chip_beside = swap(chip, "y")
+    end = chips_z - 1
+    streams = []
+    for s in range(2):
+        both = chip[:, :, s * HD : (s + 1) * HD]
+        streams.append(dict(both=both, mine={}, across={}, beside={}, corner={}))
     for k in range(1, chips_z):
-        low = k & -k
-        if k == 2:
-            mine[0], normed = tie((mine[0], normed))
-        mine[k] = along_z(mine[k - low], low)
-        if k == 2:
-            tied = (mine[k], across[1], beside[1], chip_beside, normed, ints_all, ints_other)
-            tied = tie(tied)
-            mine[k], across[1], beside[1], chip_beside, normed, ints_all, ints_other = tied
-            normed_other = swap(normed, "core")
-        elif k == 3:
-            mine[k], beside[2], normed_other = tie((mine[k], beside[2], normed_other))
-        elif k > 3:
-            mine[k], beside[k - 1] = tie((mine[k], beside[k - 1]))
-        across[k], beside[k] = swap(mine[k], "x"), swap(mine[k], "y")
-    end = chips_z - 1
-    for k in range(1, chips_z):
-        corner[k] = swap(across[k], "y") if k == end else swap(beside[k], "x")
+        for s, stream in enumerate(streams):
+            mine, across, beside = stream["mine"], stream["across"], stream["beside"]
+            if k == 1:
+                if s == 1:
+                    tied = (stream["both"], streams[0]["mine"][1])
+                    stream["both"], streams[0]["mine"][1] = tie(tied)
+                mine[0] = lax.dynamic_index_in_dim(stream["both"], x, 0, keepdims=False)
+                stream["far"] = swap(stream["both"], "y")
+            mine[k] = lax.ppermute(mine[k - 1], "z", ring)
+            if k == 2:
+                mine[k], across[1], stream["far"], first = tie(
+                    (mine[k], across[1], stream["far"], streams[1]["mine"][1])
+                )
+                if s == 0:
+                    tied = (mine[k], first, normed, ints_all, ints_other)
+                    mine[k], first, normed, ints_all, ints_other = tie(tied)
+                    normed_other = swap(normed, "core")
+                    streams[1]["mine"][1] = first
+            elif k > 2:
+                tied = (mine[k], across[k - 1], beside[k - 1], beside[k - 2])
+                mine[k], across[k - 1], beside[k - 1], beside[k - 2] = tie(tied)
+            across[k], beside[k] = swap(mine[k], "x"), swap(mine[k], "y")
+    for stream in streams:
+        for k in range(1, chips_z):
+            stream["corner"][k] = (
+                swap(stream["beside"][k], "x") if k % 2 else swap(stream["across"][k], "y")
+            )
 
     where = jnp.concatenate([position[0], ints_other[1]]).astype(jnp.float32)
     half = HD // 2
@@ -277,54 +280,57 @@
         name="mask",
     )(*ints_all)
 
-    place = jnp.stack([z, y, x]).astype(jnp.int32)
-    acc_shape = jax.ShapeDtypeStruct((2, 2 * count, 2 * HD), jnp.float32)
-    kv_shape = jax.ShapeDtypeStruct((count, 4 * HD), bf16)
-    final = [(end - 1, False)]
-    late = [(end, True)] + [(k, False) for k in range(1, chips_z) if k != end - 1]
+    spot = sum(jnp.where(z == order[i], i, 0) for i in range(chips_z))
+    place = jnp.stack([y, x, spot]).astype(jnp.int32)
+    acc_shape = jax.ShapeDtypeStruct((2 * count, 2 * HD), jnp.float32)
+    kv_shape = jax.ShapeDtypeStruct((count, 2 * HD), bf16)
+    final = [(end, False)]
+    late = [(end, True)] + [(k, False) for k in range(1, end)]
     early = [(0, True), (0, False)] + [(k, True) for k in range(1, end)]
-    acc = []
-    for groups in (early, late, final):
-        first, last = groups is early, groups is final
-        arrays = []
-        for k, near in groups:
-            if k == 0:
-                arrays.append(chip if near else chip_beside)
-            else:
-                arrays += [mine[k], across[k]] if near else [beside[k], corner[k]]
-        anywhere = pl.BlockSpec(memory_space=pl.ANY)
-        outs = pl.pallas_call(
-            functools.partial(project_kernel, groups, first, last, count),
-            out_shape=[kv_shape] * 2 if last else [acc_shape],
-            in_specs=[pl.BlockSpec(memory_space=pltpu.SMEM)]
-            + [anywhere] * (2 + len(arrays))
-            + [whole] * (len(acc) + (3 if last else 0)),
-            out_specs=[whole] * (2 if last else 1),
-            scratch_shapes=[
-                pltpu.VMEM((len(groups), 2, rows, 2 * HD), bf16),
-                pltpu.VMEM((len(groups), 2 * count, rows), bf16),
-                pltpu.SemaphoreType.DMA((len(groups), 4)),
-            ],
-            compiler_params=params,
-            cost_estimate=pl.CostEstimate(
-                flops=2 * 2 * count * rows * 4 * HD * len(groups),
-                bytes_accessed=2 * rows * (4 * HD + 2 * count) * len(groups),
-                transcendentals=0,
-            ),
-            name="project",
-        )(
-            place, normed, normed_other, *arrays, *acc,
-            *((cosine, sine, key_gain[None]) if last else ()),
-        )
-        acc = [outs[-1]]
-
-    kv_own, kv_other = outs
+    in_hbm = pl.BlockSpec(memory_space=pltpu.HBM)
     result = None
-    for cross, kv in enumerate((kv_own, kv_other)):
-        sources = [kv if d == 0 and not cross else along_ctx(kv, d, cross) for d in range(m)]
-
-        def block(step, place, needs, cross=cross):
-            return (0, lax.rem(place[0] + cross, 2) * 2 + step)
+    for s, stream in enumerate(streams):
+        acc = []
+        for groups in (early, late, final):
+            first, last = groups is early, groups is final
+            arrays = []
+            for k, near in groups:
+                if k == 0:
+                    arrays.append(stream["both" if near else "far"])
+                else:
+                    kinds = ("mine", "across") if near else ("beside", "corner")
+                    arrays += [stream[kind][k] for kind in kinds]
+            outs = pl.pallas_call(
+                functools.partial(project_kernel, groups, first, last, count),
+                out_shape=[kv_shape] * 2 if last else [acc_shape],
+                in_specs=[pl.BlockSpec(memory_space=pltpu.SMEM)]
+                + [in_hbm] * (2 + len(arrays))
+                + [whole] * (len(acc) + (3 if last else 0)),
+                out_specs=[whole] * (2 if last else 1),
+                scratch_shapes=[
+                    pltpu.VMEM((len(groups), rows, 2 * HD), bf16),
+                    pltpu.VMEM((len(groups), 2 * count, rows), bf16),
+                    pltpu.SemaphoreType.DMA((len(groups), 4)),
+                ],
+                compiler_params=params,
+                cost_estimate=pl.CostEstimate(
+                    flops=2 * 2 * count * rows * 2 * HD * len(groups),
+                    bytes_accessed=2 * rows * (2 * HD + 2 * count) * len(groups),
+                    transcendentals=0,
+                ),
+                name="project",
+            )(
+                place, normed, normed_other, *arrays, *acc,
+                *((cosine, sine, key_gain[None]) if last else ()),
+            )
+            acc = [outs[-1]]
+
+        kv_own, kv_other = outs
+        sources = [kv_own] + [along_ctx(kv_own, d) for d in range(1, m)]
+        sources += [along_ctx(kv_other, d, True) for d in range(m)]
+
+        def block(step, place, needs, s=s):
+            return (0, lax.rem(place[0] + step, 2) * 2 + s)
 
         earlier = [] if result is None else [result]
         result = pl.pallas_call(
@@ -334,7 +340,7 @@
                 num_scalar_prefetch=2,
                 grid=(2,),
                 in_specs=[pl.BlockSpec((count, G * HD), block)]
-                + [whole] * (1 + m)
+                + [whole] * (1 + 2 * m)
                 + [pl.BlockSpec(memory_space=pl.ANY)] * len(earlier),
                 out_specs=pl.BlockSpec((count, G * HD), block),
                 scratch_shapes=[
@@ -342,7 +348,7 @@
                     pltpu.VMEM((m * count, HD), bf16),
                 ],
             ),
-            input_output_aliases={4 + m: 0} if earlier else {},
+            input_output_aliases={4 + 2 * m: 0} if earlier else {},
             compiler_params=params,
             cost_estimate=pl.CostEstimate(
                 flops=2 * count * m * count * KVH * G * HD,

time: 92 us -> 99.4 us (1.080)
  waiting for transfers between devices: 35.6 us -> 16.6 us
  starting transfers between devices: 23.9 us -> 41.1 us
  Pallas kernels: 23.1 us -> 31.5 us
    ppermute x13 -> x23, starting transfers between devices: 15.1 us -> 25.4 us  [swap(): return lax.ppermute(array, axis, [(0, 1), (1, 0)])]
    ppermute x4 -> x7, waiting for transfers between devices: 9.59 us -> 0.15 us  [along_ctx(): return lax.ppermute(array, ('core', 'ctx', 'x'), pairs)]
    ppermute x13 -> x23, waiting for transfers between devices: 15.1 us -> 6.41 us  [swap(): return lax.ppermute(array, axis, [(0, 1), (1, 0)])]
    pallas_call x3 -> x6, Pallas kernels: 10.2 us -> 18.6 us  [on_device(): pl.pallas_call(functools.partial(project_kernel, groups, first, last, cou...]
    ppermute x3 -> x6, starting transfers between devices: 6.02 us -> 10.7 us  [on_device(): mine[k] = lax.ppermute(mine[k - 1], 'z', ring)]
    ppermute x4 -> x7, starting transfers between devices: 2.81 us -> 5.02 us  [along_ctx(): return lax.ppermute(array, ('core', 'ctx', 'x'), pairs)]
    ppermute x3 -> x6, waiting for transfers between devices: 11 us -> 10.1 us  [on_device(): mine[k] = lax.ppermute(mine[k - 1], 'z', ring)]
    unnamed x30 -> x34, local copies, waits for them, and re-layouts: 6.12 us -> 6.48 us
  transfers between devices with their start and end apart: 20 -> 36, of which waited for: 9 -> 10; matrix products, arithmetic and copies ran while one was open for 2% -> 1% of each run, Pallas kernels for 17% -> 27%
where the time goes in v1:
time: 99.4 us; the launch traced here: 98.9 us
  starting transfers between devices  41.1 us (41%)
  Pallas kernels  31.5 us (32%)
  waiting for transfers between devices  16.6 us (17%)
  local copies, waits for them, and re-layouts  7.89 us (8%)
  other arithmetic  1.42 us (1%)
    ppermute x23, starting transfers between devices, swap(): return lax.ppermute(array, axis, [(0, 1), (1, 0)])  25.4 us
    pallas_call x6, Pallas kernels, on_device(): pl.pallas_call(functools.partial(project_kernel, groups, first, last, cou...  18.6 us
    ppermute x6, starting transfers between devices, on_device(): mine[k] = lax.ppermute(mine[k - 1], 'z', ring)  10.7 us
    ppermute x6, waiting for transfers between devices, on_device(): mine[k] = lax.ppermute(mine[k - 1], 'z', ring)  10.1 us
    pallas_call x2, Pallas kernels, on_device(): pl.pallas_call(functools.partial(attend_kernel, m, count), out_shape=jax....  9.63 us
    unnamed x34, local copies, waits for them, and re-layouts  6.48 us
    ppermute x23, waiting for transfers between devices, swap(): return lax.ppermute(array, axis, [(0, 1), (1, 0)])  6.41 us
    ppermute x7, starting transfers between devices, along_ctx(): return lax.ppermute(array, ('core', 'ctx', 'x'), pairs)  5.02 us
  transfers between devices with their start and end apart: 36, of which 10 were waited for; matrix products, arithmetic and copies ran while one was open for 1% of the time, Pallas kernels for 27%

profile of v1, /device:TPU:0, one launch (start us, length us, event | category | flops | bytes accessed | tf_op | source)
XLA Modules:
  0.0 98.9 jit_solution(6273448362405408436)
XLA Ops:
  0.0 1.2 %dynamic-slice_bitcast_fusion.2 = (bf16[1,320,256]{2,1,0:T(8,128)(2,1)S(1)}, bf16[1,320,256]{2,1,0:T(8,128)(2,1)S(1)}, bf16[1,320,256]{2,1,0:T(8,128)(2,1)S(1)}, bf16[1,320,256]{2,1,0:T(8,128)(2,1)S(1)}) fusion(bf16[320,512]{1,0:T(8,128)(2,1)} %param.14, s32[]{:T(128)S(6)} %select_n.32, s32[]{:T(128)S(6)} %select_n.30, bf16[320,512]{1,0:T(8,128)(2,1)} %param.13), kind=kLoop, calls=%fused_computation.8 | loop fusion | bytes 1310728 | tf_op jit(solution)/shard_map/stack | solution.py:197
  1.9 1.2 %collective-permute-done = bf16[2,320,256]{2,1,0:T(8,128)(2,1)S(1)} collective-permute-done((bf16[2,320,256]{2,1,0:T(8,128)(2,1)S(1)}, bf16[2,320,256]{2,1,0:T(8,128)(2,1)S(1)}, u32[]{:S(2)}, u32[]{:S(2)}) %collective-permute-start) | collective-permute-done | bytes 327712 | tf_op jit(solution)/shard_map/ppermute | solution.py:170
  3.2 3.0 %collective-permute-start.1 = (bf16[640,128]{1,0:T(8,128)(2,1)S(1)}, bf16[640,128]{1,0:T(8,128)(2,1)}, u32[]{:S(2)}, u32[]{:S(2)}) collective-permute-start(bf16[640,128]{1,0:T(8,128)(2,1)S(1)} %dynamic-slice_bitcast_fusion.1), channel_id=1, source_target_pairs={{0,8},{8,24},{24,16},{16,0},{1,9},{9,25},{25,17},{17,1},{2,10},{10... | collective-permute-start | bytes 491528 | tf_op jit(solution)/shard_map/ppermute | solution.py:244
  6.2 1.5 %collective-permute-start.4 = (bf16[2,640,128]{2,1,0:T(8,128)(2,1)S(1)}, bf16[2,640,128]{2,1,0:T(8,128)(2,1)S(1)}, u32[]{:S(2)}, u32[]{:S(2)}) collective-permute-start(bf16[2,640,128]{2,1,0:T(8,128)(2,1)S(1)} %get-tuple-element.71.rest_0_), channel_id=1, source_target_pairs={{0,4},{4,0},{1,5},{5,1},{2,6},{6,2},{3,7},{7,3},{8,12},{12,8},{9,1... | collective-permute-start | bytes 983048 | tf_op jit(solution)/shard_map/ppermute | solution.py:170
  7.7 4.1 %collective-permute-done.1.rest_2_ = bf16[640,128]{1,0:T(8,128)(2,1)} collective-permute-done((bf16[640,128]{1,0:T(8,128)(2,1)S(1)}, bf16[640,128]{1,0:T(8,128)(2,1)}, u32[]{:S(2)}, u32[]{:S(2)}) %collective-permute-start.1) | collective-permute-done | bytes 163872 | tf_op jit(solution)/shard_map/ppermute | solution.py:244
  11.8 0.7 collective-permute-start.2
  12.6 1.5 %collective-permute-start.3 = (bf16[640,128]{1,0:T(8,128)(2,1)}, bf16[640,128]{1,0:T(8,128)(2,1)S(1)}, u32[]{:S(2)}, u32[]{:S(2)}) collective-permute-start(bf16[640,128]{1,0:T(8,128)(2,1)} %collective-permute-done.1.rest_2_), channel_id=1, source_target_pairs={{0,1},{1,0},{2,3},{3,2},{4,5},{5,4},{6,7},{7,6},{8,9},{9,8},{10,11... | collective-permute-start | bytes 491528 | tf_op jit(solution)/shard_map/ppermute | solution.py:170
  14.1 3.5 %collective-permute-start.5 = (bf16[640,128]{1,0:T(8,128)(2,1)S(1)}, bf16[640,128]{1,0:T(8,128)(2,1)S(1)}, u32[]{:S(2)}, u32[]{:S(2)}) collective-permute-start(bf16[640,128]{1,0:T(8,128)(2,1)S(1)} %dynamic-slice_bitcast_fusion), channel_id=1, source_target_pairs={{0,8},{8,24},{24,16},{16,0},{1,9},{9,25},{25,17},{17,1},{2,10},{10... | collective-permute-start | bytes 491528 | tf_op jit(solution)/shard_map/ppermute | solution.py:244
  18.2 1.9 %collective-permute-done.2.rest_4_ = bf16[640,128]{1,0:T(8,128)(2,1)} collective-permute-done((bf16[640,128]{1,0:T(8,128)(2,1)}, bf16[640,128]{1,0:T(8,128)(2,1)}, u32[]{:S(2)}, u32[]{:S(2)}) %collective-permute-start.2) | collective-permute-done | bytes 163872 | tf_op jit(solution)/shard_map/ppermute | solution.py:244
  20.2 1.7 %copy-done.1 = bf16[1,256,5120]{2,1,0:T(8,128)(2,1)S(1)} copy-done((bf16[1,256,5120]{2,1,0:T(8,128)(2,1)S(1)}, bf16[1,256,5120]{2,1,0:T(8,128)(2,1)}, u32[]{:S(2)}) %copy-start.1) | copy-done | bytes 2621464
  21.9 2.4 %norm.1.own = bf16[8,256,640]{2,1,0:T(8,128)(2,1)S(1)} custom-call(bf16[256,5120]{1,0:T(8,128)(2,1)S(1)} %bitcast.25, f32[1,5120]{1,0:T(1,128)S(1)} %bitcast.26), custom_call_target="tpu_custom_call" | custom-call | flops 5242880 | bytes 5242880 | tf_op jit(solution)/shard_map/norm/pallas_call | solution.py:208
  25.0 0.7 copy-done.2
  26.3 1.6 %collective-permute-start.11 = (bf16[2,640,128]{2,1,0:T(8,128)(2,1)S(1)}, bf16[2,640,128]{2,1,0:T(8,128)(2,1)S(1)}, u32[]{:S(2)}, u32[]{:S(2)}) collective-permute-start(bf16[2,640,128]{2,1,0:T(8,128)(2,1)S(1)} %get-tuple-element.40.rest_0_), channel_id=1, source_target_pairs={{0,4},{4,0},{1,5},{5,1},{2,6},{6,2},{3,7},{7,3},{8,12},{12,8},{9,1... | collective-permute-start | bytes 983048 | tf_op jit(solution)/shard_map/ppermute | solution.py:170
  27.9 0.8 collective-permute-start.9
  28.7 1.5 %collective-permute-start.10 = (bf16[640,128]{1,0:T(8,128)(2,1)S(1)}, bf16[640,128]{1,0:T(8,128)(2,1)S(1)}, u32[]{:S(2)}, u32[]{:S(2)}) collective-permute-start(bf16[640,128]{1,0:T(8,128)(2,1)S(1)} %collective-permute-done.5.rest_2_), channel_id=1, source_target_pairs={{0,1},{1,0},{2,3},{3,2},{4,5},{5,4},{6,7},{7,6},{8,9},{9,8},{10,11... | collective-permute-start | bytes 491528 | tf_op jit(solution)/shard_map/ppermute | solution.py:170
  30.7 4.0 %collective-permute-done.9.rest_4_ = bf16[640,128]{1,0:T(8,128)(2,1)S(1)} collective-permute-done((bf16[640,128]{1,0:T(8,128)(2,1)S(1)}, bf16[640,128]{1,0:T(8,128)(2,1)S(1)}, u32[]{:S(2)}, u32[]{:S(2)}) %collective-permute-start.9) | collective-permute-done | bytes 163872 | tf_op jit(solution)/shard_map/ppermute | solution.py:244
  34.7 0.8 collective-permute-start.24
  36.2 1.5 %collective-permute-start.25 = (bf16[640,128]{1,0:T(8,128)(2,1)}, bf16[640,128]{1,0:T(8,128)(2,1)}, u32[]{:S(2)}, u32[]{:S(2)}) collective-permute-start(bf16[640,128]{1,0:T(8,128)(2,1)} %collective-permute-done.2.rest_4_), channel_id=1, source_target_pairs={{0,1},{1,0},{2,3},{3,2},{4,5},{5,4},{6,7},{7,6},{8,9},{9,8},{10,11... | collective-permute-start | bytes 491528 | tf_op jit(solution)/shard_map/ppermute | solution.py:170
  37.7 0.7 copy-done.4
  38.4 0.8 collective-permute-start.26
  39.6 2.3 %collective-permute-start.15 = (bf16[640,128]{1,0:T(8,128)(2,1)S(1)}, bf16[640,128]{1,0:T(8,128)(2,1)S(1)}, u32[]{:S(2)}, u32[]{:S(2)}) collective-permute-start(bf16[640,128]{1,0:T(8,128)(2,1)S(1)} %collective-permute-done.5.rest_2_), channel_id=1, source_target_pairs={{0,4},{4,0},{1,5},{5,1},{2,6},{6,2},{3,7},{7,3},{8,12},{12,8},{9,1... | collective-permute-start | bytes 491528 | tf_op jit(solution)/shard_map/ppermute | solution.py:170
  41.9 1.9 %collective-permute-start.12 = (bf16[640,128]{1,0:T(8,128)(2,1)}, bf16[640,128]{1,0:T(8,128)(2,1)S(1)}, u32[]{:S(2)}, u32[]{:S(2)}) collective-permute-start(bf16[640,128]{1,0:T(8,128)(2,1)} %copy-done.6), channel_id=1, source_target_pairs={{0,8},{8,24},{24,16},{16,0},{1,9},{9,25},{25,17},{17,1},{2,10},{10... | collective-permute-start | bytes 491528 | tf_op jit(solution)/shard_map/ppermute | solution.py:244
  44.3 0.9 collective-permute-done.26.rest_4_
  45.3 1.2 %collective-permute-start.14 = (bf16[640,128]{1,0:T(8,128)(2,1)}, bf16[640,128]{1,0:T(8,128)(2,1)S(1)}, u32[]{:S(2)}, u32[]{:S(2)}) collective-permute-start(bf16[640,128]{1,0:T(8,128)(2,1)} %copy-done.6), channel_id=1, source_target_pairs={{0,4},{4,0},{1,5},{5,1},{2,6},{6,2},{3,7},{7,3},{8,12},{12,8},{9,1... | collective-permute-start | bytes 491528 | tf_op jit(solution)/shard_map/ppermute | solution.py:170
  46.6 2.1 %collective-permute-done.15.rest_2_ = bf16[640,128]{1,0:T(8,128)(2,1)S(1)} collective-permute-done((bf16[640,128]{1,0:T(8,128)(2,1)S(1)}, bf16[640,128]{1,0:T(8,128)(2,1)S(1)}, u32[]{:S(2)}, u32[]{:S(2)}) %collective-permute-start.15) | collective-permute-done | bytes 163872 | tf_op jit(solution)/shard_map/ppermute | solution.py:170
  48.7 1.2 %collective-permute-start.28 = (bf16[640,128]{1,0:T(8,128)(2,1)}, bf16[640,128]{1,0:T(8,128)(2,1)S(1)}, u32[]{:S(2)}, u32[]{:S(2)}) collective-permute-start(bf16[640,128]{1,0:T(8,128)(2,1)} %collective-permute-done.24.rest_0_), channel_id=1, source_target_pairs={{0,4},{4,0},{1,5},{5,1},{2,6},{6,2},{3,7},{7,3},{8,12},{12,8},{9,1... | collective-permute-start | bytes 491528 | tf_op jit(solution)/shard_map/ppermute | solution.py:170
  49.9 1.5 %collective-permute-start.30 = (bf16[640,128]{1,0:T(8,128)(2,1)}, bf16[640,128]{1,0:T(8,128)(2,1)S(1)}, u32[]{:S(2)}, u32[]{:S(2)}) collective-permute-start(bf16[640,128]{1,0:T(8,128)(2,1)} %collective-permute-done.24.rest_0_), channel_id=1, source_target_pairs={{0,1},{1,0},{2,3},{3,2},{4,5},{5,4},{6,7},{7,6},{8,9},{9,8},{10,11... | collective-permute-start | bytes 491528 | tf_op jit(solution)/shard_map/ppermute | solution.py:170
  52.6 1.2 %collective-permute-start.32 = (bf16[640,128]{1,0:T(8,128)(2,1)}, bf16[640,128]{1,0:T(8,128)(2,1)S(1)}, u32[]{:S(2)}, u32[]{:S(2)}) collective-permute-start(bf16[640,128]{1,0:T(8,128)(2,1)} %collective-permute-done.25.rest_5_), channel_id=1, source_target_pairs={{0,4},{4,0},{1,5},{5,1},{2,6},{6,2},{3,7},{7,3},{8,12},{12,8},{9,1... | collective-permute-start | bytes 491528 | tf_op jit(solution)/shard_map/ppermute | solution.py:170
  53.9 1.0 %fusion = (f32[512,64]{1,0:T(8,128)S(1)}, f32[512,64]{1,0:T(8,128)S(1)}, f32[512,64]{1,0:T(8,128)S(1)}) fusion(f32[64]{0:T(128)S(1)} %copy-done.16, f32[512]{0:T(512)S(1)} %add_convert_fusion), kind=kLoop, calls=%fused_computation.12 | loop fusion | flops 65536 | bytes 395520 | tf_op jit(solution)/shard_map/neg | solution.py:270
  55.0 1.1 %collective-permute-done.28.rest_0_ = bf16[640,128]{1,0:T(8,128)(2,1)S(1)} collective-permute-done((bf16[640,128]{1,0:T(8,128)(2,1)}, bf16[640,128]{1,0:T(8,128)(2,1)S(1)}, u32[]{:S(2)}, u32[]{:S(2)}) %collective-permute-start.28) | collective-permute-done | bytes 163872 | tf_op jit(solution)/shard_map/ppermute | solution.py:170
  56.1 1.2 %collective-permute-start.16 = (bf16[640,128]{1,0:T(8,128)(2,1)S(1)}, bf16[640,128]{1,0:T(8,128)(2,1)S(1)}, u32[]{:S(2)}, u32[]{:S(2)}) collective-permute-start(bf16[640,128]{1,0:T(8,128)(2,1)S(1)} %collective-permute-done.12.rest_0_), channel_id=1, source_target_pairs={{0,4},{4,0},{1,5},{5,1},{2,6},{6,2},{3,7},{7,3},{8,12},{12,8},{9,1... | collective-permute-start | bytes 491528 | tf_op jit(solution)/shard_map/ppermute | solution.py:170
  57.4 1.5 %collective-permute-start.18 = (bf16[640,128]{1,0:T(8,128)(2,1)S(1)}, bf16[640,128]{1,0:T(8,128)(2,1)S(1)}, u32[]{:S(2)}, u32[]{:S(2)}) collective-permute-start(bf16[640,128]{1,0:T(8,128)(2,1)S(1)} %collective-permute-done.12.rest_0_), channel_id=1, source_target_pairs={{0,1},{1,0},{2,3},{3,2},{4,5},{5,4},{6,7},{7,6},{8,9},{9,8},{10,11... | collective-permute-start | bytes 491528 | tf_op jit(solution)/shard_map/ppermute | solution.py:170
  58.9 1.4 %collective-permute-start.19 = (bf16[640,128]{1,0:T(8,128)(2,1)S(1)}, bf16[640,128]{1,0:T(8,128)(2,1)S(1)}, u32[]{:S(2)}, u32[]{:S(2)}) collective-permute-start(bf16[640,128]{1,0:T(8,128)(2,1)S(1)} %collective-permute-done.15.rest_2_), channel_id=1, source_target_pairs={{0,1},{1,0},{2,3},{3,2},{4,5},{5,4},{6,7},{7,6},{8,9},{9,8},{10,11... | collective-permute-start | bytes 491528 | tf_op jit(solution)/shard_map/ppermute | solution.py:170
  60.3 0.9 collective-permute-start.29
  61.3 1.6 %collective-permute-start.20 = (bf16[640,128]{1,0:T(8,128)(2,1)S(1)}, bf16[640,128]{1,0:T(8,128)(2,1)S(1)}, u32[]{:S(2)}, u32[]{:S(2)}) collective-permute-start(bf16[640,128]{1,0:T(8,128)(2,1)S(1)} %collective-permute-done.13.rest_5_), channel_id=1, source_target_pairs={{0,4},{4,0},{1,5},{5,1},{2,6},{6,2},{3,7},{7,3},{8,12},{12,8},{9,1... | collective-permute-start | bytes 491528 | tf_op jit(solution)/shard_map/ppermute | solution.py:170
  62.9 1.0 copy-done.3
  63.9 0.9 copy-done.9
  64.8 3.8 %project.9.rest_6_ = f32[512,256]{1,0:T(8,128)S(1)} custom-call(s32[3]{0:T(128)S(1)} %pad_add_fusion.1.place, bf16[8,256,640]{2,1,0:T(8,128)(2,1)S(1)} %norm.1.own, bf16[8,256,640]{2,1,0:T(8,128)(2,1)} %collective-permute-done.8.other, bf16[2,640,128]{2,1,0:T(8,128)(2,1)S(1)} %get-tuple-element.71.rest_0_, bf16[2,640,128]{2,1,0:T(8,128)(2,1)S(1)} %copy-done.3, ...), custom_call_target="tpu_custom_call" | custom-call | flops 671088640 | bytes 3932160 | tf_op jit(solution)/shard_map/project/pallas_call | solution.py:303
  68.8 3.1 %project.10.rest_2_ = f32[512,256]{1,0:T(8,128)S(1)} custom-call(s32[3]{0:T(128)S(1)} %pad_add_fusion.1.place, bf16[8,256,640]{2,1,0:T(8,128)(2,1)S(1)} %norm.1.own, bf16[8,256,640]{2,1,0:T(8,128)(2,1)} %collective-permute-done.8.other, bf16[640,128]{1,0:T(8,128)(2,1)} %collective-permute-done.24.rest_0_, ...), custom_call_target="tpu_custom_call" | custom-call | flops 503316480 | bytes 2949120 | tf_op jit(solution)/shard_map/project/pallas_call | solution.py:303
  72.0 2.5 %project.11 = (bf16[256,256]{1,0:T(8,128)(2,1)S(1)}, bf16[256,256]{1,0:T(8,128)(2,1)S(1)}) custom-call(s32[3]{0:T(128)S(1)} %pad_add_fusion.1.place, bf16[8,256,640]{2,1,0:T(8,128)(2,1)S(1)} %norm.1.own, bf16[8,256,640]{2,1,0:T(8,128)(2,1)} %collective-permute-done.8.other, bf16[640,128]{1,0:T(8,128)(2,1)S(1)} %collective-permute-done.28.rest_0_, ...), custom_call_target="tpu_custom_call" | custom-call | flops 167772160 | bytes 983040 | tf_op jit(solution)/shard_map/project/pallas_call | solution.py:303
  74.5 2.0 %collective-permute-start.33 = (bf16[256,256]{1,0:T(8,128)(2,1)S(1)}, bf16[256,256]{1,0:T(8,128)(2,1)S(1)}, u32[]{:S(2)}, u32[]{:S(2)}) collective-permute-start(bf16[256,256]{1,0:T(8,128)(2,1)S(1)} %get-tuple-element.69.rest_0_), channel_id=1, source_target_pairs={{0,1},{1,0},{2,3},{3,2},{4,5},{5,4},{6,7},{7,6},{8,9},{9,8},{10,11... | collective-permute-start | bytes 393224 | tf_op jit(solution)/shard_map/ppermute | solution.py:193
  76.7 3.7 %project.6.rest_6_ = f32[512,256]{1,0:T(8,128)S(1)} custom-call(s32[3]{0:T(128)S(1)} %pad_add_fusion.1.place, bf16[8,256,640]{2,1,0:T(8,128)(2,1)S(1)} %norm.1.own, bf16[8,256,640]{2,1,0:T(8,128)(2,1)} %collective-permute-done.8.other, bf16[2,640,128]{2,1,0:T(8,128)(2,1)S(1)} %get-tuple-element.40.rest_0_, bf16[2,640,128]{2,1,0:T(8,128)(2,1)S(1)} %copy-done.5, ...), custom_call_target="tpu_custom_call" | custom-call | flops 671088640 | bytes 3932160 | tf_op jit(solution)/shard_map/project/pallas_call | solution.py:303
  80.4 3.1 %project.7.rest_2_ = f32[512,256]{1,0:T(8,128)S(1)} custom-call(s32[3]{0:T(128)S(1)} %pad_add_fusion.1.place, bf16[8,256,640]{2,1,0:T(8,128)(2,1)S(1)} %norm.1.own, bf16[8,256,640]{2,1,0:T(8,128)(2,1)} %collective-permute-done.8.other, bf16[640,128]{1,0:T(8,128)(2,1)S(1)} %collective-permute-done.12.rest_0_, ...), custom_call_target="tpu_custom_call" | custom-call | flops 503316480 | bytes 2949120 | tf_op jit(solution)/shard_map/project/pallas_call | solution.py:303
  83.5 2.5 %project.8 = (bf16[256,256]{1,0:T(8,128)(2,1)S(1)}, bf16[256,256]{1,0:T(8,128)(2,1)S(1)}) custom-call(s32[3]{0:T(128)S(1)} %pad_add_fusion.1.place, bf16[8,256,640]{2,1,0:T(8,128)(2,1)S(1)} %norm.1.own, bf16[8,256,640]{2,1,0:T(8,128)(2,1)} %collective-permute-done.8.other, bf16[640,128]{1,0:T(8,128)(2,1)S(1)} %collective-permute-done.16.rest_0_, ...), custom_call_target="tpu_custom_call" | custom-call | flops 167772160 | bytes 983040 | tf_op jit(solution)/shard_map/project/pallas_call | solution.py:303
  86.0 2.0 %collective-permute-start.21 = (bf16[256,256]{1,0:T(8,128)(2,1)S(1)}, bf16[256,256]{1,0:T(8,128)(2,1)S(1)}, u32[]{:S(2)}, u32[]{:S(2)}) collective-permute-start(bf16[256,256]{1,0:T(8,128)(2,1)S(1)} %get-tuple-element.60.rest_0_), channel_id=1, source_target_pairs={{0,1},{1,0},{2,3},{3,2},{4,5},{5,4},{6,7},{7,6},{8,9},{9,8},{10,11... | collective-permute-start | bytes 393224 | tf_op jit(solution)/shard_map/ppermute | solution.py:193
  88.2 0.9 mask.1
  89.1 4.7 %attend.2.rest_4_ = bf16[256,4096]{1,0:T(8,128)(2,1)} custom-call(s32[1]{0:T(128)} %bitcast.place, s32[2]{0:T(128)S(1)} %get-tuple-element.48.needs, bf16[256,4096]{1,0:T(8,128)(2,1)S(1)} %bitcast.23, f32[256,512]{1,0:T(8,128)S(1)} %get-tuple-element.49.bias, bf16[256,256]{1,0:T(8,128)(2,1)S(1)} %get-tuple-element.69.rest_0_, ...), custom_call_target="tpu_custom_call" | custom-call | flops 1073741824 | bytes 2097152 | tf_op jit(solution)/shard_map/attend/pallas_call | solution.py:336
  94.0 4.9 %attend.3 = bf16[256,4096]{1,0:T(8,128)(2,1)} custom-call(s32[1]{0:T(128)} %bitcast.place, s32[2]{0:T(128)S(1)} %get-tuple-element.48.needs, bf16[256,4096]{1,0:T(8,128)(2,1)S(1)} %bitcast.24, f32[256,512]{1,0:T(8,128)S(1)} %get-tuple-element.49.bias, bf16[256,256]{1,0:T(8,128)(2,1)S(1)} %get-tuple-element.60.rest_0_, ...), custom_call_target="tpu_custom_call", output_to_operand_aliasing={{}: (8, {})} | custom-call | flops 1073741824 | bytes 2097152 | tf_op jit(solution)/shard_map/attend/pallas_call | solution.py:336
  (83 shorter events, 7.2 us)
Async XLA Ops:
  1.2 16.4 %copy-start.14 = (s32[1,256]{1,0:T(1,128)S(1)}, s32[1,256]{1,0:T(1,128)}, u32[]{:S(2)}) copy-start(s32[1,256]{1,0:T(1,128)} %param.16) | copy-start | bytes 3076
  1.2 16.4 %copy-start.15 = (s32[1,256]{1,0:T(1,128)S(1)}, s32[1,256]{1,0:T(1,128)}, u32[]{:S(2)}) copy-start(s32[1,256]{1,0:T(1,128)} %param.15) | copy-start | bytes 3076
  1.2 19.0 %copy-start.12 = (f32[5120]{0:T(1024)S(1)}, f32[5120]{0:T(1024)}, u32[]{:S(2)}) copy-start(f32[5120]{0:T(1024)} %param.11) | copy-start | bytes 61444
  1.3 1.8 %collective-permute-start = (bf16[2,320,256]{2,1,0:T(8,128)(2,1)S(1)}, bf16[2,320,256]{2,1,0:T(8,128)(2,1)S(1)}, u32[]{:S(2)}, u32[]{:S(2)}) collective-permute-start(bf16[2,320,256]{2,1,0:T(8,128)(2,1)S(1)} %pad_maximum_fusion), channel_id=1, source_target_pairs={{0,2},{2,0},{1,3},{3,1},{4,6},{6,4},{5,7},{7,5},{8,10},{10,8},{9,1... | collective-permute-start | bytes 983048 | tf_op jit(solution)/shard_map/ppermute | solution.py:170
  3.2 8.6 %collective-permute-start.1 = (bf16[640,128]{1,0:T(8,128)(2,1)S(1)}, bf16[640,128]{1,0:T(8,128)(2,1)}, u32[]{:S(2)}, u32[]{:S(2)}) collective-permute-start(bf16[640,128]{1,0:T(8,128)(2,1)S(1)} %dynamic-slice_bitcast_fusion.1), channel_id=1, source_target_pairs={{0,8},{8,24},{24,16},{16,0},{1,9},{9,25},{25,17},{17,1},{2,10},{10... | collective-permute-start | bytes 491528 | tf_op jit(solution)/shard_map/ppermute | solution.py:244
  6.2 18.8 %collective-permute-start.4 = (bf16[2,640,128]{2,1,0:T(8,128)(2,1)S(1)}, bf16[2,640,128]{2,1,0:T(8,128)(2,1)S(1)}, u32[]{:S(2)}, u32[]{:S(2)}) collective-permute-start(bf16[2,640,128]{2,1,0:T(8,128)(2,1)S(1)} %get-tuple-element.71.rest_0_), channel_id=1, source_target_pairs={{0,4},{4,0},{1,5},{5,1},{2,6},{6,2},{3,7},{7,3},{8,12},{12,8},{9,1... | collective-permute-start | bytes 983048 | tf_op jit(solution)/shard_map/ppermute | solution.py:170
  11.8 8.3 %collective-permute-start.2 = (bf16[640,128]{1,0:T(8,128)(2,1)}, bf16[640,128]{1,0:T(8,128)(2,1)}, u32[]{:S(2)}, u32[]{:S(2)}) collective-permute-start(bf16[640,128]{1,0:T(8,128)(2,1)} %collective-permute-done.1.rest_2_), channel_id=1, source_target_pairs={{0,8},{8,24},{24,16},{16,0},{1,9},{9,25},{25,17},{17,1},{2,10},{10... | collective-permute-start | bytes 491528 | tf_op jit(solution)/shard_map/ppermute | solution.py:244
  12.6 11.7 %collective-permute-start.3 = (bf16[640,128]{1,0:T(8,128)(2,1)}, bf16[640,128]{1,0:T(8,128)(2,1)S(1)}, u32[]{:S(2)}, u32[]{:S(2)}) collective-permute-start(bf16[640,128]{1,0:T(8,128)(2,1)} %collective-permute-done.1.rest_2_), channel_id=1, source_target_pairs={{0,1},{1,0},{2,3},{3,2},{4,5},{5,4},{6,7},{7,6},{8,9},{9,8},{10,11... | collective-permute-start | bytes 491528 | tf_op jit(solution)/shard_map/ppermute | solution.py:170
  14.1 11.6 %collective-permute-start.5 = (bf16[640,128]{1,0:T(8,128)(2,1)S(1)}, bf16[640,128]{1,0:T(8,128)(2,1)S(1)}, u32[]{:S(2)}, u32[]{:S(2)}) collective-permute-start(bf16[640,128]{1,0:T(8,128)(2,1)S(1)} %dynamic-slice_bitcast_fusion), channel_id=1, source_target_pairs={{0,8},{8,24},{24,16},{16,0},{1,9},{9,25},{25,17},{17,1},{2,10},{10... | collective-permute-start | bytes 491528 | tf_op jit(solution)/shard_map/ppermute | solution.py:244
  17.6 8.1 %collective-permute-start.6 = (s32[2,256]{1,0:T(2,128)S(1)}, s32[2,256]{1,0:T(2,128)S(1)}, u32[]{:S(2)}, u32[]{:S(2)}) collective-permute-start(s32[2,256]{1,0:T(2,128)S(1)} %pad_add_fusion.refs_0_), channel_id=1, source_target_pairs={{0,1},{1,0},{2,3},{3,2},{4,5},{5,4},{6,7},{7,6},{8,9},{9,8},{10,11... | collective-permute-start | bytes 6152 | tf_op jit(solution)/shard_map/ppermute | solution.py:193
  20.2 5.6 %collective-permute-start.7 = (s32[2,256]{1,0:T(2,128)S(1)}, s32[2,256]{1,0:T(2,128)S(1)}, u32[]{:S(2)}, u32[]{:S(2)}) collective-permute-start(s32[2,256]{1,0:T(2,128)S(1)} %pad_add_fusion.refs_0_), channel_id=1, source_target_pairs={{0,2},{2,0},{1,3},{3,1},{4,6},{6,4},{5,7},{7,5},{8,10},{10,8},{9,1... | collective-permute-start | bytes 6152 | tf_op jit(solution)/shard_map/ppermute | solution.py:170
  20.2 1.7 %copy-start.1 = (bf16[1,256,5120]{2,1,0:T(8,128)(2,1)S(1)}, bf16[1,256,5120]{2,1,0:T(8,128)(2,1)}, u32[]{:S(2)}) copy-start(bf16[1,256,5120]{2,1,0:T(8,128)(2,1)} %param.9) | copy-start | bytes 7864324
  21.9 31.9 %copy-start.16 = (f32[64]{0:T(128)S(1)}, f32[64]{0:T(128)}, u32[]{:S(2)}) copy-start(f32[64]{0:T(128)} %constant.47) | copy-start | bytes 772
  25.7 35.6 %collective-permute-start.8 = (bf16[8,256,640]{2,1,0:T(8,128)(2,1)S(1)}, bf16[8,256,640]{2,1,0:T(8,128)(2,1)}, u32[]{:S(2)}, u32[]{:S(2)}) collective-permute-start(bf16[8,256,640]{2,1,0:T(8,128)(2,1)S(1)} %norm.1.own), channel_id=1, source_target_pairs={{0,2},{2,0},{1,3},{3,1},{4,6},{6,4},{5,7},{7,5},{8,10},{10,8},{9,1... | collective-permute-start | bytes 7864328 | tf_op jit(solution)/shard_map/ppermute | solution.py:170
  26.3 11.3 %collective-permute-start.11 = (bf16[2,640,128]{2,1,0:T(8,128)(2,1)S(1)}, bf16[2,640,128]{2,1,0:T(8,128)(2,1)S(1)}, u32[]{:S(2)}, u32[]{:S(2)}) collective-permute-start(bf16[2,640,128]{2,1,0:T(8,128)(2,1)S(1)} %get-tuple-element.40.rest_0_), channel_id=1, source_target_pairs={{0,4},{4,0},{1,5},{5,1},{2,6},{6,2},{3,7},{7,3},{8,12},{12,8},{9,1... | collective-permute-start | bytes 983048 | tf_op jit(solution)/shard_map/ppermute | solution.py:170
  27.9 6.8 %collective-permute-start.9 = (bf16[640,128]{1,0:T(8,128)(2,1)S(1)}, bf16[640,128]{1,0:T(8,128)(2,1)S(1)}, u32[]{:S(2)}, u32[]{:S(2)}) collective-permute-start(bf16[640,128]{1,0:T(8,128)(2,1)S(1)} %collective-permute-done.5.rest_2_), channel_id=1, source_target_pairs={{0,8},{8,24},{24,16},{16,0},{1,9},{9,25},{25,17},{17,1},{2,10},{10... | collective-permute-start | bytes 491528 | tf_op jit(solution)/shard_map/ppermute | solution.py:244
  28.7 6.8 %collective-permute-start.10 = (bf16[640,128]{1,0:T(8,128)(2,1)S(1)}, bf16[640,128]{1,0:T(8,128)(2,1)S(1)}, u32[]{:S(2)}, u32[]{:S(2)}) collective-permute-start(bf16[640,128]{1,0:T(8,128)(2,1)S(1)} %collective-permute-done.5.rest_2_), channel_id=1, source_target_pairs={{0,1},{1,0},{2,3},{3,2},{4,5},{5,4},{6,7},{7,6},{8,9},{9,8},{10,11... | collective-permute-start | bytes 491528 | tf_op jit(solution)/shard_map/ppermute | solution.py:170
  30.2 9.4 %collective-permute-start.27 = (bf16[640,128]{1,0:T(8,128)(2,1)}, bf16[640,128]{1,0:T(8,128)(2,1)}, u32[]{:S(2)}, u32[]{:S(2)}) collective-permute-start(bf16[640,128]{1,0:T(8,128)(2,1)} %collective-permute-done.1.rest_2_), channel_id=1, source_target_pairs={{0,4},{4,0},{1,5},{5,1},{2,6},{6,2},{3,7},{7,3},{8,12},{12,8},{9,1... | collective-permute-start | bytes 491528 | tf_op jit(solution)/shard_map/ppermute | solution.py:170
  34.7 3.0 %copy-start.6 = (bf16[640,128]{1,0:T(8,128)(2,1)}, bf16[640,128]{1,0:T(8,128)(2,1)S(1)}, u32[]{:S(2)}) copy-start(bf16[640,128]{1,0:T(8,128)(2,1)S(1)} %collective-permute-done.9.rest_4_) | copy-start | bytes 491524
  34.7 7.2 %collective-permute-start.24 = (bf16[640,128]{1,0:T(8,128)(2,1)}, bf16[640,128]{1,0:T(8,128)(2,1)}, u32[]{:S(2)}, u32[]{:S(2)}) collective-permute-start(bf16[640,128]{1,0:T(8,128)(2,1)} %collective-permute-done.2.rest_4_), channel_id=1, source_target_pairs={{0,8},{8,24},{24,16},{16,0},{1,9},{9,25},{25,17},{17,1},{2,10},{10... | collective-permute-start | bytes 491528 | tf_op jit(solution)/shard_map/ppermute | solution.py:244
  36.2 7.6 %collective-permute-start.25 = (bf16[640,128]{1,0:T(8,128)(2,1)}, bf16[640,128]{1,0:T(8,128)(2,1)}, u32[]{:S(2)}, u32[]{:S(2)}) collective-permute-start(bf16[640,128]{1,0:T(8,128)(2,1)} %collective-permute-done.2.rest_4_), channel_id=1, source_target_pairs={{0,1},{1,0},{2,3},{3,2},{4,5},{5,4},{6,7},{7,6},{8,9},{9,8},{10,11... | collective-permute-start | bytes 491528 | tf_op jit(solution)/shard_map/ppermute | solution.py:170
  38.4 6.9 %collective-permute-start.26 = (bf16[640,128]{1,0:T(8,128)(2,1)}, bf16[640,128]{1,0:T(8,128)(2,1)}, u32[]{:S(2)}, u32[]{:S(2)}) collective-permute-start(bf16[640,128]{1,0:T(8,128)(2,1)} %collective-permute-done.2.rest_4_), channel_id=1, source_target_pairs={{0,4},{4,0},{1,5},{5,1},{2,6},{6,2},{3,7},{7,3},{8,12},{12,8},{9,1... | collective-permute-start | bytes 491528 | tf_op jit(solution)/shard_map/ppermute | solution.py:170
  39.6 9.0 %collective-permute-start.15 = (bf16[640,128]{1,0:T(8,128)(2,1)S(1)}, bf16[640,128]{1,0:T(8,128)(2,1)S(1)}, u32[]{:S(2)}, u32[]{:S(2)}) collective-permute-start(bf16[640,128]{1,0:T(8,128)(2,1)S(1)} %collective-permute-done.5.rest_2_), channel_id=1, source_target_pairs={{0,4},{4,0},{1,5},{5,1},{2,6},{6,2},{3,7},{7,3},{8,12},{12,8},{9,1... | collective-permute-start | bytes 491528 | tf_op jit(solution)/shard_map/ppermute | solution.py:170
  41.9 8.0 %collective-permute-start.12 = (bf16[640,128]{1,0:T(8,128)(2,1)}, bf16[640,128]{1,0:T(8,128)(2,1)S(1)}, u32[]{:S(2)}, u32[]{:S(2)}) collective-permute-start(bf16[640,128]{1,0:T(8,128)(2,1)} %copy-done.6), channel_id=1, source_target_pairs={{0,8},{8,24},{24,16},{16,0},{1,9},{9,25},{25,17},{17,1},{2,10},{10... | collective-permute-start | bytes 491528 | tf_op jit(solution)/shard_map/ppermute | solution.py:244
  43.8 7.6 %collective-permute-start.13 = (bf16[640,128]{1,0:T(8,128)(2,1)}, bf16[640,128]{1,0:T(8,128)(2,1)S(1)}, u32[]{:S(2)}, u32[]{:S(2)}) collective-permute-start(bf16[640,128]{1,0:T(8,128)(2,1)} %copy-done.6), channel_id=1, source_target_pairs={{0,1},{1,0},{2,3},{3,2},{4,5},{5,4},{6,7},{7,6},{8,9},{9,8},{10,11... | collective-permute-start | bytes 491528 | tf_op jit(solution)/shard_map/ppermute | solution.py:170
  45.3 7.3 %collective-permute-start.14 = (bf16[640,128]{1,0:T(8,128)(2,1)}, bf16[640,128]{1,0:T(8,128)(2,1)S(1)}, u32[]{:S(2)}, u32[]{:S(2)}) collective-permute-start(bf16[640,128]{1,0:T(8,128)(2,1)} %copy-done.6), channel_id=1, source_target_pairs={{0,4},{4,0},{1,5},{5,1},{2,6},{6,2},{3,7},{7,3},{8,12},{12,8},{9,1... | collective-permute-start | bytes 491528 | tf_op jit(solution)/shard_map/ppermute | solution.py:170
  48.7 7.5 %collective-permute-start.28 = (bf16[640,128]{1,0:T(8,128)(2,1)}, bf16[640,128]{1,0:T(8,128)(2,1)S(1)}, u32[]{:S(2)}, u32[]{:S(2)}) collective-permute-start(bf16[640,128]{1,0:T(8,128)(2,1)} %collective-permute-done.24.rest_0_), channel_id=1, source_target_pairs={{0,4},{4,0},{1,5},{5,1},{2,6},{6,2},{3,7},{7,3},{8,12},{12,8},{9,1... | collective-permute-start | bytes 491528 | tf_op jit(solution)/shard_map/ppermute | solution.py:170
  49.9 7.5 %collective-permute-start.30 = (bf16[640,128]{1,0:T(8,128)(2,1)}, bf16[640,128]{1,0:T(8,128)(2,1)S(1)}, u32[]{:S(2)}, u32[]{:S(2)}) collective-permute-start(bf16[640,128]{1,0:T(8,128)(2,1)} %collective-permute-done.24.rest_0_), channel_id=1, source_target_pairs={{0,1},{1,0},{2,3},{3,2},{4,5},{5,4},{6,7},{7,6},{8,9},{9,8},{10,11... | collective-permute-start | bytes 491528 | tf_op jit(solution)/shard_map/ppermute | solution.py:170
  51.4 7.5 %collective-permute-start.31 = (bf16[640,128]{1,0:T(8,128)(2,1)}, bf16[640,128]{1,0:T(8,128)(2,1)S(1)}, u32[]{:S(2)}, u32[]{:S(2)}) collective-permute-start(bf16[640,128]{1,0:T(8,128)(2,1)} %collective-permute-done.27.rest_2_), channel_id=1, source_target_pairs={{0,1},{1,0},{2,3},{3,2},{4,5},{5,4},{6,7},{7,6},{8,9},{9,8},{10,11... | collective-permute-start | bytes 491528 | tf_op jit(solution)/shard_map/ppermute | solution.py:170
  52.6 7.7 %collective-permute-start.32 = (bf16[640,128]{1,0:T(8,128)(2,1)}, bf16[640,128]{1,0:T(8,128)(2,1)S(1)}, u32[]{:S(2)}, u32[]{:S(2)}) collective-permute-start(bf16[640,128]{1,0:T(8,128)(2,1)} %collective-permute-done.25.rest_5_), channel_id=1, source_target_pairs={{0,4},{4,0},{1,5},{5,1},{2,6},{6,2},{3,7},{7,3},{8,12},{12,8},{9,1... | collective-permute-start | bytes 491528 | tf_op jit(solution)/shard_map/ppermute | solution.py:170
  56.1 12.5 %collective-permute-start.16 = (bf16[640,128]{1,0:T(8,128)(2,1)S(1)}, bf16[640,128]{1,0:T(8,128)(2,1)S(1)}, u32[]{:S(2)}, u32[]{:S(2)}) collective-permute-start(bf16[640,128]{1,0:T(8,128)(2,1)S(1)} %collective-permute-done.12.rest_0_), channel_id=1, source_target_pairs={{0,4},{4,0},{1,5},{5,1},{2,6},{6,2},{3,7},{7,3},{8,12},{12,8},{9,1... | collective-permute-start | bytes 491528 | tf_op jit(solution)/shard_map/ppermute | solution.py:170
  57.4 19.1 %collective-permute-start.18 = (bf16[640,128]{1,0:T(8,128)(2,1)S(1)}, bf16[640,128]{1,0:T(8,128)(2,1)S(1)}, u32[]{:S(2)}, u32[]{:S(2)}) collective-permute-start(bf16[640,128]{1,0:T(8,128)(2,1)S(1)} %collective-permute-done.12.rest_0_), channel_id=1, source_target_pairs={{0,1},{1,0},{2,3},{3,2},{4,5},{5,4},{6,7},{7,6},{8,9},{9,8},{10,11... | collective-permute-start | bytes 491528 | tf_op jit(solution)/shard_map/ppermute | solution.py:170
  58.9 17.6 %collective-permute-start.19 = (bf16[640,128]{1,0:T(8,128)(2,1)S(1)}, bf16[640,128]{1,0:T(8,128)(2,1)S(1)}, u32[]{:S(2)}, u32[]{:S(2)}) collective-permute-start(bf16[640,128]{1,0:T(8,128)(2,1)S(1)} %collective-permute-done.15.rest_2_), channel_id=1, source_target_pairs={{0,1},{1,0},{2,3},{3,2},{4,5},{5,4},{6,7},{7,6},{8,9},{9,8},{10,11... | collective-permute-start | bytes 491528 | tf_op jit(solution)/shard_map/ppermute | solution.py:170
  60.3 11.7 %collective-permute-start.29 = (bf16[640,128]{1,0:T(8,128)(2,1)S(1)}, bf16[640,128]{1,0:T(8,128)(2,1)S(1)}, u32[]{:S(2)}, u32[]{:S(2)}) collective-permute-start(bf16[640,128]{1,0:T(8,128)(2,1)S(1)} %collective-permute-done.28.rest_0_), channel_id=1, source_target_pairs={{0,1},{1,0},{2,3},{3,2},{4,5},{5,4},{6,7},{7,6},{8,9},{9,8},{10,11... | collective-permute-start | bytes 491528 | tf_op jit(solution)/shard_map/ppermute | solution.py:170
  61.3 19.1 %collective-permute-start.20 = (bf16[640,128]{1,0:T(8,128)(2,1)S(1)}, bf16[640,128]{1,0:T(8,128)(2,1)S(1)}, u32[]{:S(2)}, u32[]{:S(2)}) collective-permute-start(bf16[640,128]{1,0:T(8,128)(2,1)S(1)} %collective-permute-done.13.rest_5_), channel_id=1, source_target_pairs={{0,4},{4,0},{1,5},{5,1},{2,6},{6,2},{3,7},{7,3},{8,12},{12,8},{9,1... | collective-permute-start | bytes 491528 | tf_op jit(solution)/shard_map/ppermute | solution.py:170
  62.9 1.0 copy-start.3
  68.7 3.3 %copy-start.13 = (f32[128]{0:T(128)S(1)}, f32[128]{0:T(128)}, u32[]{:S(2)}) copy-start(f32[128]{0:T(128)} %param.12) | copy-start | bytes 1540
  68.7 14.8 %collective-permute-start.17 = (bf16[640,128]{1,0:T(8,128)(2,1)S(1)}, bf16[640,128]{1,0:T(8,128)(2,1)S(1)}, u32[]{:S(2)}, u32[]{:S(2)}) collective-permute-start(bf16[640,128]{1,0:T(8,128)(2,1)S(1)} %collective-permute-done.16.rest_0_), channel_id=1, source_target_pairs={{0,1},{1,0},{2,3},{3,2},{4,5},{5,4},{6,7},{7,6},{8,9},{9,8},{10,11... | collective-permute-start | bytes 491528 | tf_op jit(solution)/shard_map/ppermute | solution.py:170
  72.0 4.7 %copy-start.5 = (bf16[2,640,128]{2,1,0:T(8,128)(2,1)S(1)}, bf16[2,640,128]{2,1,0:T(8,128)(2,1)}, u32[]{:S(2)}) copy-start(bf16[2,640,128]{2,1,0:T(8,128)(2,1)} %copy-done.4) | copy-start | bytes 983044
  72.0 4.7 %copy-start.7 = (bf16[640,128]{1,0:T(8,128)(2,1)S(1)}, bf16[640,128]{1,0:T(8,128)(2,1)}, u32[]{:S(2)}) copy-start(bf16[640,128]{1,0:T(8,128)(2,1)} %copy-done.6) | copy-start | bytes 491524
  72.0 4.7 %copy-start.11 = (bf16[640,128]{1,0:T(8,128)(2,1)S(1)}, bf16[640,128]{1,0:T(8,128)(2,1)}, u32[]{:S(2)}) copy-start(bf16[640,128]{1,0:T(8,128)(2,1)} %copy-done.10) | copy-start | bytes 491524
  74.5 13.5 %collective-permute-start.33 = (bf16[256,256]{1,0:T(8,128)(2,1)S(1)}, bf16[256,256]{1,0:T(8,128)(2,1)S(1)}, u32[]{:S(2)}, u32[]{:S(2)}) collective-permute-start(bf16[256,256]{1,0:T(8,128)(2,1)S(1)} %get-tuple-element.69.rest_0_), channel_id=1, source_target_pairs={{0,1},{1,0},{2,3},{3,2},{4,5},{5,4},{6,7},{7,6},{8,9},{9,8},{10,11... | collective-permute-start | bytes 393224 | tf_op jit(solution)/shard_map/ppermute | solution.py:193
  76.5 12.6 %collective-permute-start.34 = (bf16[256,256]{1,0:T(8,128)(2,1)S(1)}, bf16[256,256]{1,0:T(8,128)(2,1)S(1)}, u32[]{:S(2)}, u32[]{:S(2)}) collective-permute-start(bf16[256,256]{1,0:T(8,128)(2,1)S(1)} %get-tuple-element.70), channel_id=1, source_target_pairs={{0,2},{1,3},{2,0},{3,1},{4,6},{5,7},{6,4},{7,5},{8,10},{9,11},{10,... | collective-permute-start | bytes 393224 | tf_op jit(solution)/shard_map/ppermute | solution.py:193
  76.5 12.6 %collective-permute-start.35 = (bf16[256,256]{1,0:T(8,128)(2,1)S(1)}, bf16[256,256]{1,0:T(8,128)(2,1)S(1)}, u32[]{:S(2)}, u32[]{:S(2)}) collective-permute-start(bf16[256,256]{1,0:T(8,128)(2,1)S(1)} %get-tuple-element.70), channel_id=1, source_target_pairs={{0,3},{1,2},{2,1},{3,0},{4,7},{5,6},{6,5},{7,4},{8,11},{9,10},{10,... | collective-permute-start | bytes 393224 | tf_op jit(solution)/shard_map/ppermute | solution.py:193
  83.5 5.6 %copy-start = (bf16[1,256,4096]{2,1,0:T(8,128)(2,1)S(1)}, bf16[1,256,4096]{2,1,0:T(8,128)(2,1)}, u32[]{:S(2)}) copy-start(bf16[1,256,4096]{2,1,0:T(8,128)(2,1)} %param.10) | copy-start | bytes 6291460
  86.0 7.8 %collective-permute-start.21 = (bf16[256,256]{1,0:T(8,128)(2,1)S(1)}, bf16[256,256]{1,0:T(8,128)(2,1)S(1)}, u32[]{:S(2)}, u32[]{:S(2)}) collective-permute-start(bf16[256,256]{1,0:T(8,128)(2,1)S(1)} %get-tuple-element.60.rest_0_), channel_id=1, source_target_pairs={{0,1},{1,0},{2,3},{3,2},{4,5},{5,4},{6,7},{7,6},{8,9},{9,8},{10,11... | collective-permute-start | bytes 393224 | tf_op jit(solution)/shard_map/ppermute | solution.py:193
  88.0 5.8 %collective-permute-start.22 = (bf16[256,256]{1,0:T(8,128)(2,1)S(1)}, bf16[256,256]{1,0:T(8,128)(2,1)S(1)}, u32[]{:S(2)}, u32[]{:S(2)}) collective-permute-start(bf16[256,256]{1,0:T(8,128)(2,1)S(1)} %get-tuple-element.61), channel_id=1, source_target_pairs={{0,2},{1,3},{2,0},{3,1},{4,6},{5,7},{6,4},{7,5},{8,10},{9,11},{10,... | collective-permute-start | bytes 393224 | tf_op jit(solution)/shard_map/ppermute | solution.py:193
  88.0 6.0 %collective-permute-start.23 = (bf16[256,256]{1,0:T(8,128)(2,1)S(1)}, bf16[256,256]{1,0:T(8,128)(2,1)S(1)}, u32[]{:S(2)}, u32[]{:S(2)}) collective-permute-start(bf16[256,256]{1,0:T(8,128)(2,1)S(1)} %get-tuple-element.61), channel_id=1, source_target_pairs={{0,3},{1,2},{2,1},{3,0},{4,7},{5,6},{6,5},{7,4},{8,11},{9,10},{10,... | collective-permute-start | bytes 393224 | tf_op jit(solution)/shard_map/ppermute | solution.py:193
  (5 other events, 3.7 us)
